TPU v7x, 32 devices: a whole 2x2x4 slice. The times are simulated.
32 devices in a mesh: grp: 2 (over core), row: 4 (over y, x), col: 4 (over z).
Axes of the slice: x: 2, y: 2, z: 4, core: 2. Of those that a mesh axis runs over, the one named last changes fastest.
Arguments:
- global_state: bfloat16 [64, 1440, 384], P(('grp', 'row'), 'col'), may hold values from -6 to 6
- spec_filter: float32 [2, 720, 384], P(None, None, 'col'), may hold values from -4 to 4
- w_skip: bfloat16 [384, 384], replicated, may hold values from -0.3125 to 0.3125
- w_mix: bfloat16 [384, 384], replicated, may hold values from -0.3125 to 0.3125
- w_decode: bfloat16 [384, 26], replicated, may hold values from -0.3125 to 0.3125
- regional_state: bfloat16 [99, 128, 512], P(None, ('grp', 'row'), 'col'), may hold values from -6 to 6
- noise_draws: bfloat16 [2, 99, 128, 512], P(None, None, ('grp', 'row'), 'col'), may hold values from -6 to 6
- w_first: bfloat16 [128, 9, 125], replicated, may hold values from -0.1875 to 0.1875
- w_down: bfloat16 [256, 9, 128], replicated, may hold values from -0.1875 to 0.1875
- w_up: bfloat16 [128, 256], replicated, may hold values from -0.375 to 0.375
- w_bridge: bfloat16 [128, 128], replicated, may hold values from -0.5 to 0.5
- w_last: bfloat16 [99, 9, 128], replicated, may hold values from -0.1875 to 0.1875
- box_lat0: int32 [1], replicated, may hold values from 0 to 46
- box_lon0: int32 [1], replicated, may hold values from 0 to 1374
- stencil_lat: int32 [128, 512], P(('grp', 'row'), 'col'), may hold values from 0 to 16, as said below
- stencil_lon: int32 [128, 512], P(('grp', 'row'), 'col'), may hold values from 0 to 64, as said below
Outputs:
- global_final: bfloat16 [64, 1440, 384], P(('grp', 'row'), 'col')
- regional_final: bfloat16 [99, 128, 512], P(None, ('grp', 'row'), 'col')
Inputs may be any that keep to these rules, and one draw needn't show every extreme that they name: stencil_lat[r, q] is r // 8 or r // 8 + 1. stencil_lon[r, q] is q // 8 or q // 8 + 1.
All inputs are finite; a program needn't handle non-finite values.
Results may differ from a plain program's by a relative error of at most 0.012.
Values may be sent and summed in bfloat16 or wider, within the bound.
No kernel may reach another device: no remote copies, remote signals or barrier semaphores. Data moves between devices by JAX's collectives and lax.ppermute only.
A program may use at most 128 MiB of HBM per device.

v0:
```python
import functools
import math

import jax
import jax.numpy as jnp
import ml_dtypes
import numpy as np
from jax import lax
from jax.experimental import pallas as pl
from jax.experimental.pallas import tpu as pltpu
from jax.sharding import PartitionSpec as P

RATIO = 8
noise_level = 0.5
PLANE = ("grp", "row")
RIM = 9
RIM_USED = 4
LANES = 128
VMEM = 60 * 2**20
PACKED = 32
MODE_TILE = 64
STRIP = 8
FAR = -4096
RIM_COLS = 16


def fourier_tables(length, num_modes):
    position = np.arange(length, dtype=np.int64)[:, None]
    frequency = np.arange(num_modes, dtype=np.int64)[None, :]
    angle = (position * frequency % length).astype(np.float64) * (2.0 * math.pi / length)
    cosine = np.cos(angle)
    sine = np.sin(angle)
    factor = np.where(frequency == 0, 1.0, 2.0) / length
    forward = np.concatenate([cosine, -sine], axis=1).T.astype(ml_dtypes.bfloat16)
    inverse = np.concatenate([cosine * factor, -sine * factor], axis=1).astype(ml_dtypes.bfloat16)
    return forward, inverse


def round_up(size, unit):
    return -(-size // unit) * unit


def split_tables(length, num_modes):
    piece = length // 4
    place = np.arange(piece, dtype=np.int64)[:, None]

    def waves(mode):
        angle = (place * mode[None, :] % length).astype(np.float64) * (2.0 * math.pi / length)
        return np.cos(angle), np.sin(angle), np.where(mode == 0, 1.0, 2.0)[None, :] / length

    def padded(blocks, unit_rows, unit_cols):
        rows = []
        for row in blocks:
            cols = []
            for block in row:
                spare = [(0, -block.shape[0] % unit_rows), (0, -block.shape[1] % unit_cols)]
                cols.append(np.pad(block, spare))
            rows.append(np.concatenate(cols, axis=1))
        return np.concatenate(rows, axis=0).astype(ml_dtypes.bfloat16)

    forward, inverse = [], []
    for residue in (0, 2):
        cosine, sine, factor = waves(np.arange(residue, num_modes, 4))
        forward.append(padded([[cosine.T], [-sine.T]], MODE_TILE, LANES))
        inverse.append(padded([[cosine * factor, -sine * factor]], LANES, MODE_TILE))
    mode = np.arange(1, num_modes, 2)
    cosine, sine, factor = waves(mode)
    sign = np.where(mode % 4 == 1, 1.0, -1.0)[None, :]
    odd_forward = padded(
        [[cosine.T, (-sign * sine).T], [-sine.T, (-sign * cosine).T]], 2 * MODE_TILE, LANES
    )
    odd_inverse = padded(
        [
            [cosine * factor, -sine * factor],
            [-sign * sine * factor, -sign * cosine * factor],
        ],
        LANES,
        2 * MODE_TILE,
    )
    return tuple(
        jnp.asarray(table)
        for table in (np.stack(forward), odd_forward, np.stack(inverse), odd_inverse)
    )


def exchange(blocks, axis):
    return lax.all_to_all(blocks, axis, split_axis=0, concat_axis=0, tiled=True)


def spread(block, axis):
    return exchange(jnp.broadcast_to(block[None], (lax.axis_size(axis),) + block.shape), axis)


def filter_share(spec_filter):
    rows = 2 * spec_filter.shape[1]
    flat = spec_filter.reshape(rows, spec_filter.shape[2])
    share = rows // lax.axis_size(PLANE)
    mine = lax.dynamic_slice_in_dim(flat, lax.axis_index(PLANE) * share, share, 0)
    return mine.astype(jnp.bfloat16)


def every_channel(mine):
    count = lax.axis_size("col")
    me = lax.axis_index("col")
    blocks = [shift(mine, "col", -step) if step else mine for step in range(count)]
    ring = jnp.concatenate(blocks + blocks[:-1], axis=1)
    width = mine.shape[1]
    return lax.dynamic_slice_in_dim(ring, (count - me) % count * width, count * width, 1)


def gelu(x):
    slope = math.sqrt(2.0 / math.pi)
    half = 0.5 * x
    return half + half * jnp.tanh(x * (slope + (0.044715 * slope) * (x * x)))


def latitude_kernel(hours, turns, step, place_ref, *refs):
    piece_refs, refs = refs[:4], refs[4:]
    even_forward_ref, odd_forward_ref = refs[:2]
    far_refs, out_refs, strip_ref, refs = refs[2:8], refs[8:12], refs[12], refs[13:]
    near_refs, sems, refs = refs[:6], refs[6], refs[7:]
    filter_ref, even_inverse_ref, odd_inverse_ref, skip_ref, mix_ref, decode_ref = near_refs
    state_ref, gain_ref, coarse_ref, near_ref, packed_ref = refs
    copies = [
        pltpu.make_async_copy(far, near, sems.at[index])
        for index, (far, near) in enumerate(zip(far_refs, near_refs))
    ]
    for copy in copies:
        copy.start()
    f32, bf16 = jnp.float32, jnp.bfloat16
    piece, channels = piece_refs[0].shape[1:]
    padded = state_ref.shape[0] // 4
    group = LANES // PACKED
    span = near_ref.shape[0]
    rows = span // group
    spare = jnp.zeros((padded - piece, channels), bf16)
    for index in range(4):
        for turn in range(turns):
            state_ref[
                index * padded : (index + 1) * padded, turn * channels : (turn + 1) * channels
            ] = jnp.concatenate([piece_refs[index][turn], spare], axis=0)

    modes = filter_ref.shape[0] // 2

    def spread_gains():
        for index in range(channels // LANES):
            lanes = slice(index * LANES, (index + 1) * LANES)
            gain_ref[index, : 2 * modes, :] = filter_ref[:, lanes].astype(f32)
            gain_ref[index, 2 * modes :, :] = jnp.zeros((gain_ref.shape[1] - 2 * modes, LANES), f32)

    def gain_rows(low, count, stride):
        rows = pl.ds(low, count, stride=stride)
        tiles = [gain_ref[index, rows, :] for index in range(channels // LANES)]
        return jnp.concatenate(tiles * turns, axis=1)

    def gain(spectrum, low, stride):
        half = spectrum.shape[0] // 2
        real, imag = spectrum[:half], spectrum[half:]
        gain_real = gain_rows(low, half, stride)
        gain_imag = gain_rows(modes + low, half, stride)
        return jnp.concatenate(
            [
                (real * gain_real - imag * gain_imag).astype(bf16),
                (real * gain_imag + imag * gain_real).astype(bf16),
            ],
            axis=0,
        )

    def dot(left, right):
        return jnp.dot(left, right, preferred_element_type=f32)

    for hour in range(hours):
        pieces = [
            state_ref[index * padded : (index + 1) * padded, :].astype(f32) for index in range(4)
        ]
        both, other = pieces[0] + pieces[2], pieces[1] + pieces[3]
        spectra = [
            dot(even_forward_ref[index], mixed.astype(bf16))
            for index, mixed in enumerate((both + other, both - other))
        ]
        mixed = jnp.concatenate([pieces[0] - pieces[2], pieces[1] - pieces[3]], axis=0)
        spectra.append(dot(odd_forward_ref[...], mixed.astype(bf16)))
        if hour == 0:
            copies[0].wait()
            spread_gains()
            for copy in copies[1:]:
                copy.wait()
        shares = [
            dot(even_inverse_ref[index], gain(spectra[index], 2 * index, 4)) for index in range(2)
        ]
        odd = dot(odd_inverse_ref[...], gain(spectra[2], 1, 2))
        for index in range(4):
            here = slice(index * padded, (index + 1) * padded)
            even = shares[0] + shares[1] if index % 2 == 0 else shares[0] - shares[1]
            part = odd[:padded] if index % 2 == 0 else odd[padded:]
            spectral = even + part if index < 2 else even - part
            for turn in range(turns):
                lanes = slice(turn * channels, (turn + 1) * channels)
                state = state_ref[here, lanes]
                activated = gelu(spectral[:, lanes] + dot(state, skip_ref[...])).astype(bf16)
                update = dot(activated, mix_ref[...])
                state_ref[here, lanes] = (state.astype(f32) + update).astype(bf16)

        for index in range(2):
            here = pl.ds(pl.multiple_of(place_ref[index] * padded, LANES), padded)
            for turn in range(turns):
                lanes = slice(turn * channels, (turn + 1) * channels)
                coarse = dot(state_ref[here, lanes], decode_ref[...])
                coarse_ref[turn, index * piece : (index + 1) * piece, :] = coarse[:piece]
        for turn in range(turns):
            near_ref[...] = coarse_ref[turn, pl.ds(place_ref[2], span), :]
            packed = near_ref[pl.ds(0, rows, stride=group), :]
            for sub in range(1, group):
                packed += pltpu.roll(near_ref[pl.ds(sub, rows, stride=group), :], sub * PACKED, 1)
            packed_ref[turn, hour * rows : (hour + 1) * rows, :] = packed

    for index in range(4):
        for turn in range(turns):
            out_refs[index][turn] = state_ref[
                index * padded : index * padded + piece, turn * channels : (turn + 1) * channels
            ]
    for target in range(4):
        low = target * step // group
        for turn in range(turns):
            strip = [
                packed_ref[turn, hour * rows + low : hour * rows + low + STRIP, :]
                for hour in range(hours)
            ]
            strip_ref[target, turn * hours * STRIP : (turn + 1) * hours * STRIP, :] = jnp.concatenate(
                strip, axis=0
            ).astype(bf16)


def advance_latitudes(hours, step, place, pieces, tables, gains, w_skip, w_mix, w_decode):
    turns, piece, channels = pieces[0].shape
    padded = round_up(piece, LANES)
    group = LANES // PACKED
    span = round_up(3 * step + STRIP * group, 8 * group)
    decode = jnp.pad(w_decode, ((0, 0), (0, LANES - w_decode.shape[1])))
    modes = gains.shape[0] // 2
    late = (gains,) + tables[2:] + (w_skip, w_mix, decode)
    spare = max(4 * (tables[0].shape[1] // 2), 2 * (tables[1].shape[0] // 2)) - modes
    results = pl.pallas_call(
        functools.partial(latitude_kernel, hours, turns, step),
        out_shape=tuple(
            jax.ShapeDtypeStruct((turns, piece, channels), jnp.bfloat16) for _ in pieces
        )
        + (jax.ShapeDtypeStruct((4, turns * hours * STRIP, LANES), jnp.bfloat16),),
        in_specs=[pl.BlockSpec(memory_space=pltpu.SMEM)]
        + [pl.BlockSpec(memory_space=pltpu.VMEM)] * 6
        + [pl.BlockSpec(memory_space=pl.ANY)] * len(late),
        scratch_shapes=[pltpu.VMEM(array.shape, array.dtype) for array in late]
        + [
            pltpu.SemaphoreType.DMA((len(late),)),
            pltpu.VMEM((4 * padded, turns * channels), jnp.bfloat16),
            pltpu.VMEM((channels // LANES, gains.shape[0] + spare, LANES), jnp.float32),
            pltpu.VMEM((turns, 2 * piece, LANES), jnp.float32),
            pltpu.VMEM((span, LANES), jnp.float32),
            pltpu.VMEM((turns, hours * span // group, LANES), jnp.float32),
        ],
        compiler_params=pltpu.CompilerParams(vmem_limit_bytes=VMEM),
        cost_estimate=pl.CostEstimate(
            flops=turns * 16 * 10**9,
            bytes_accessed=turns * 6 * 2**20,
            transcendentals=hours * turns * 4 * piece * channels,
        ),
        name="advance_latitudes",
    )(place, *pieces, *tables[:2], *late)
    return results[:4], results[4]


def collate_kernel(count, place_ref, *refs):
    pieces, out_ref, sems = refs[:count], refs[count], refs[count + 1]
    copies = [
        pltpu.make_async_copy(
            piece, out_ref.at[pl.ds(place_ref[index], piece.shape[0])], sems.at[index]
        )
        for index, piece in enumerate(pieces)
    ]
    for copy in copies:
        copy.start()
    for copy in copies:
        copy.wait()


def collate(place, pieces):
    count = len(pieces)
    turns, piece, channels = pieces[0].shape
    return pl.pallas_call(
        functools.partial(collate_kernel, count),
        out_shape=jax.ShapeDtypeStruct((count * turns, piece, channels), pieces[0].dtype),
        in_specs=[pl.BlockSpec(memory_space=pltpu.SMEM)]
        + [pl.BlockSpec(memory_space=pltpu.VMEM)] * count,
        out_specs=pl.BlockSpec(memory_space=pl.ANY),
        scratch_shapes=[pltpu.SemaphoreType.DMA((count,))],
        name="collate",
    )(place, *pieces)


def shift(block, axis, step):
    count = lax.axis_size(axis)
    return lax.ppermute(block, axis, [(source, (source + step) % count) for source in range(count)])


def global_hour(current, spec_filter, w_skip, w_mix, forward, inverse):
    longitude = lax.all_to_all(current, "col", split_axis=2, concat_axis=1, tiled=True)
    spectrum = jnp.einsum("alc,ml->amc", longitude, forward, preferred_element_type=jnp.float32)
    num_modes = spec_filter.shape[1]
    real_part = spectrum[:, :num_modes, :]
    imag_part = spectrum[:, num_modes:, :]
    filt_real = spec_filter[0][None]
    filt_imag = spec_filter[1][None]
    mixed = jnp.concatenate(
        [
            real_part * filt_real - imag_part * filt_imag,
            real_part * filt_imag + imag_part * filt_real,
        ],
        axis=1,
    ).astype(jnp.bfloat16)
    filtered = jnp.einsum("amc,lm->alc", mixed, inverse, preferred_element_type=jnp.float32).astype(
        jnp.bfloat16
    )
    spectral = lax.all_to_all(filtered, "col", split_axis=1, concat_axis=2, tiled=True)
    skipped = jnp.einsum("alc,cd->ald", current, w_skip, preferred_element_type=jnp.float32)
    activated = jax.nn.gelu(spectral.astype(jnp.float32) + skipped).astype(jnp.bfloat16)
    update = jnp.einsum("ald,de->ale", activated, w_mix, preferred_element_type=jnp.float32)
    return (current.astype(jnp.float32) + update).astype(jnp.bfloat16)


def window_extent(cells):
    return (cells + RIM - 1) // RATIO + 3 - (-RIM // RATIO)


def window_base():
    return -(-RIM // RATIO)


def global_by_latitude(
    hours, global_state, spec_filter, w_skip, w_mix, w_decode, box_lat0, box_lon0, rows_here,
    cols_here, prepare,
):
    count = lax.axis_size("col")
    me = lax.axis_index("col")
    lats_here, piece, _ = global_state.shape
    turns = lats_here // count
    tables = split_tables(piece * count, spec_filter.shape[1])
    owners = [(me - step) % count * turns for step in range(count)]
    mine = filter_share(spec_filter)
    bands = [lax.dynamic_slice_in_dim(global_state, owner, turns, 0) for owner in owners]
    bands, mine = lax.optimization_barrier((bands, mine))
    received = [shift(band, "col", -step) if step else band for step, band in enumerate(bands)]
    wide = every_channel(mine)
    parts, weights = prepare()
    gains = spread(wide, PLANE).reshape(-1, wide.shape[1])
    start = (box_lon0[0] - window_base() - me * piece) % (piece * count)
    place = jnp.stack([start // piece, (start // piece + 1) % count, start % piece]).astype(jnp.int32)
    received, weights = lax.optimization_barrier((received, weights))
    outcome, strips = advance_latitudes(
        hours, cols_here // RATIO, place, received, tables, gains, w_skip, w_mix, w_decode
    )
    strips, parts = lax.optimization_barrier((strips, parts))
    near = []
    for step in range(count):
        strip = lax.dynamic_index_in_dim(strips, (me - step) % count, 0, keepdims=False)
        near.append(shift(strip, "col", -step) if step else strip)
    near, outcome = lax.optimization_barrier((jnp.stack(near), outcome))
    got = spread(near, PLANE)
    plane = lax.axis_size(PLANE)
    got = got.reshape((plane * lats_here, -1, LANES))
    lat = box_lat0[0] - window_base() + lax.axis_index(PLANE) * (rows_here // RATIO)
    lat = jnp.clip(lat + jnp.arange(window_extent(rows_here), dtype=jnp.int32), 0, plane * lats_here - 1)
    band, lat = lat // lats_here, lat % lats_here
    pick = (band * count + (lat // turns - me) % count) * turns + lat % turns
    finals = [shift(block, "col", step) if step else block for step, block in enumerate(outcome)]

    def finish(after):
        blocks, after = lax.optimization_barrier((finals, after))
        return collate(jnp.stack(owners).astype(jnp.int32), blocks), after

    return finish, got, pick.astype(jnp.int32), (parts, weights)


def global_by_channel(
    hours, global_state, spec_filter, w_skip, w_mix, w_decode, box_lat0, box_lon0, rows_here,
    cols_here, prepare,
):
    count = lax.axis_size("col")
    prepared = prepare()
    forward, inverse = fourier_tables(global_state.shape[1] * count, spec_filter.shape[1])
    base = window_base()
    high, wide = window_extent(rows_here), window_extent(cols_here)
    span = (count - 1) * (cols_here // RATIO) + wide
    lat_start = box_lat0[0] + lax.axis_index(PLANE) * (rows_here // RATIO)
    lon_start = box_lon0[0] + lax.axis_index("col") * (cols_here // RATIO)
    windows = []
    for _ in range(hours):
        global_state = global_hour(global_state, spec_filter, w_skip, w_mix, forward, inverse)
        coarse = jnp.einsum(
            "alc,ck->alk", global_state, w_decode, preferred_element_type=jnp.float32
        ).astype(jnp.bfloat16)
        coarse = lax.all_gather(coarse, "col", axis=1, tiled=True)
        coarse = jnp.pad(coarse, ((0, 0), (base, span), (0, 0)))
        coarse = lax.dynamic_slice_in_dim(coarse, box_lon0[0], base + span, 1)
        coarse = lax.all_gather(coarse, PLANE, axis=0, tiled=True)
        coarse = lax.dynamic_slice_in_dim(coarse, lon_start - box_lon0[0], wide, 1)
        coarse = jnp.pad(coarse, ((base, high), (0, 0), (0, 0)))
        coarse = lax.dynamic_slice_in_dim(coarse, lat_start, high, 0)
        windows.append(coarse)
    group = LANES // PACKED
    windows = jnp.stack(windows, axis=1)
    windows = jnp.pad(
        windows, ((0, 0), (0, 0), (0, STRIP * group - wide), (0, PACKED - windows.shape[3]))
    )
    windows = windows.reshape(high, hours * STRIP, LANES)
    return lambda after: (global_state, after), windows, jnp.arange(high, dtype=jnp.int32), prepared


def next_to(low, high, axis):
    count = lax.axis_size(axis)
    forward = [(i, i + 1) for i in range(count - 1)]
    backward = [(target, source) for source, target in forward]
    return lax.ppermute(low, axis, forward), lax.ppermute(high, axis, backward)


def grid_place(start_ref, total, base, extent):
    place = start_ref + base + lax.broadcasted_iota(jnp.int32, (extent, 1), 0)
    return (place >= 0) & (place < total)


def denoise_kernel(
    rows, cols, totals, variables, conds, width, place_ref, pick_ref, mid0_ref, mid1_ref, above_ref,
    below_ref, left_ref, right_ref, strip_ref, *refs
):
    far_refs, out_ref, refs = refs[:5], refs[5], refs[6:]
    near_refs, sems, refs = refs[:5], refs[5], refs[6:]
    first_w_ref, down_w_ref, up_w_ref, bridge_w_ref, last_w_ref = near_refs
    noisy_ref, noise_ref, blend_ref, own_ref, stack_ref, first_ref, pooled_ref, third_ref, pair_ref, spread_ref, window_ref = refs
    copies = [
        pltpu.make_async_copy(far, near, sems.at[index])
        for index, (far, near) in enumerate(zip(far_refs, near_refs))
    ]
    for copy in copies:
        copy.start()
    half = width // 2
    pad = (width - cols) // 2
    channels = mid0_ref.shape[2]
    f32, bf16 = jnp.float32, jnp.bfloat16

    inner = RIM - RIM_USED
    for ref, mid_ref, rim, part in ((noisy_ref, mid0_ref, RIM, 0), (noise_ref, mid1_ref, inner, RIM)):
        ref[0:rim, pad : pad + cols, :] = above_ref[part : part + rim]
        ref[rim : rim + rows, pad : pad + cols, :] = mid_ref[...]
        ref[rim + rows :, pad : pad + cols, :] = below_ref[part : part + rim]
        skip = RIM - rim
        for side_ref, low, to in ((left_ref, 0, pad - rim), (right_ref, pad + cols, 0)):
            side = side_ref[skip : skip + rows + 2 * rim].astype(f32)
            side = pltpu.roll(side, (to - part) % pad, 1)
            ref[:, low : low + pad, :] = side.astype(bf16)

    is_in = grid_place(place_ref[1], totals[1], -pad, width)
    col_in = is_in.astype(f32)
    base = window_base()
    col = lax.broadcasted_iota(jnp.int32, (width, 1), 0) - pad
    frac_col = ((col % RATIO).astype(f32) + 0.5) / RATIO
    col_base = jnp.where(is_in, (col + pad) // RATIO - pad // RATIO + base, FAR).astype(f32) + frac_col
    group = LANES // PACKED
    high = pick_ref.shape[0]
    point = lax.broadcasted_iota(jnp.int32, (1, group * high * STRIP), 1)
    point_lat = (point // STRIP % high).astype(f32)
    point_lon = (point % STRIP * group + point // (STRIP * high)).astype(f32)

    def blend(row):
        whole = row // RATIO
        frac_row = (row - whole * RATIO + 0.5) / RATIO
        there = place_ref[0] + row
        row_base = jnp.where((there >= 0) & (there < totals[0]), whole + base + frac_row, float(FAR))
        shifts = noisy_ref[row + RIM].astype(f32)
        lat = row_base + shifts[:, variables + conds : variables + conds + 1]
        lon = col_base + shifts[:, variables + conds + 1 : variables + conds + 2]
        weight_lat = jnp.maximum(1.0 - jnp.abs(point_lat - lat), 0.0)
        weight_lon = jnp.maximum(1.0 - jnp.abs(point_lon - lon), 0.0)
        return (weight_lat * weight_lon).astype(bf16)

    edges = [jnp.broadcast_to(col_in[low : low + pad], (pad, channels)) for low in (0, pad + cols)]
    lane = lax.broadcasted_iota(jnp.int32, (1, channels), 1)
    is_state = lane < variables
    is_cond = (lane >= variables) & (lane < variables + conds)
    strips = [strip_ref[pick_ref[index]].astype(f32) for index in range(high)]
    for hour in range(2):
        near = jnp.concatenate([s[hour * STRIP : (hour + 1) * STRIP] for s in strips], axis=0)
        for turn in range(LANES // PACKED):
            moved = pltpu.roll(near, (variables - turn * PACKED) % LANES, 1)
            window_ref[hour, turn * high * STRIP : (turn + 1) * high * STRIP, :] = jnp.where(
                is_cond, moved, 0.0
            ).astype(bf16)

    def flat(start, count, unit):
        return slice(start * unit, (start + count) * unit)

    def mask(value, row):
        low, mid, high = value[:pad], value[pad : pad + cols], value[pad + cols :]
        value = jnp.concatenate([low * edges[0], mid, high * edges[1]], axis=0)
        if 0 <= row < rows:
            return value
        there = place_ref[0] + row
        return value * jnp.where((there >= 0) & (there < totals[0]), 1.0, 0.0)

    def keep(ref, where, value):
        size = value.shape[0]
        ref[0, where, :] = pltpu.roll(value, 1, 0).astype(bf16)
        ref[1, where, :] = value.astype(bf16)
        ref[2, where, :] = pltpu.roll(value, size - 1, 0).astype(bf16)

    def pairs(ref, row, count):
        blocks = []
        for pair in range(count):
            taps = [
                ref[shift, flat(row + 2 * pair + step, 1, width), :]
                for step in range(4)
                for shift in range(3)
            ]
            blocks.append(jnp.concatenate(taps, axis=1))
        return jnp.concatenate(blocks, axis=0)

    def silu_of_half(half_value):
        return half_value + half_value * jnp.tanh(half_value)

    for hour in range(2):
        rim = RIM - RIM_USED * hour
        tall = rows + 2 * rim

        for row in range(0, tall, 2):
            here = flat(row, 2, width)
            if hour == 0:
                weights = jnp.concatenate([blend(row - RIM), blend(row + 1 - RIM)], axis=0)
                blend_ref[here, :] = weights
            else:
                weights = blend_ref[flat(row + RIM - rim, 2, width), :]
            cond = jnp.dot(weights, window_ref[hour], preferred_element_type=f32)
            if hour == 0:
                own = noisy_ref[row : row + 2].reshape(2 * width, channels).astype(f32)
                own_ref[here, :] = own
            else:
                own = own_ref[here, :]
            keep(stack_ref, here, jnp.where(is_state, own, cond))

        if hour == 0:
            copies[0].wait()
        for row in range(0, tall - 2, 8):
            value = jnp.dot(
                pairs(stack_ref, row, 4), first_w_ref[...], preferred_element_type=f32
            )
            for pair in range(4):
                top = row + 2 * pair
                here = flat(top // 2, 1, width)
                part = silu_of_half(value[pair * width : (pair + 1) * width])
                upper = mask(part[:, :channels], top - rim + 1)
                lower = mask(part[:, channels:], top - rim + 2)
                first_ref[here, :channels] = upper.astype(bf16)
                first_ref[here, channels:] = lower.astype(bf16)
                pair_ref[top // 2] = upper + lower
                even = pair_ref[top // 2, pl.ds(0, half, stride=2), :]
                odd = pair_ref[top // 2, pl.ds(1, half, stride=2), :]
                keep(pooled_ref, flat(top // 2, 1, half), even + odd)

        if hour == 0:
            for copy in copies[1:4]:
                copy.wait()
        half_rows = (tall - 2) // 2 - 2
        part = half_rows // 2
        for row in (0, part):
            taps = [
                pooled_ref[shift, flat(row + step, part, half), :]
                for step in range(3)
                for shift in range(3)
            ]
            second = jnp.dot(
                jnp.concatenate(taps, axis=1), down_w_ref[...], preferred_element_type=f32
            )
            lifted = jnp.dot(
                silu_of_half(second).astype(bf16), up_w_ref[...], preferred_element_type=f32
            )
            bridged = jnp.dot(
                first_ref[flat(row + 1, part, width), :], bridge_w_ref[...], preferred_element_type=f32
            )
            for step in range(part):
                own = lifted[step * half : (step + 1) * half]
                spread_ref[row + step, pl.ds(0, half, stride=2), :] = own
                spread_ref[row + step, pl.ds(1, half, stride=2), :] = own
                own = spread_ref[row + step]
                top = 2 * (row + step)
                for side in range(2):
                    value = bridged[
                        step * width : (step + 1) * width, side * channels : (side + 1) * channels
                    ]
                    value = mask(silu_of_half(value + own), top + side - rim + 3)
                    keep(third_ref, flat(top + side, 1, width), value)

        if hour == 0:
            copies[4].wait()
        skip = 1 if hour == 1 else 0
        count = (rows + 2 * (rim - RIM_USED)) // 2 if hour == 0 else rows // 2
        for first in range(0, count, 4):
            size = min(4, count - first)
            values = jnp.dot(
                pairs(third_ref, 2 * first + skip, size), last_w_ref[...], preferred_element_type=f32
            )
            for index in range(2 * size):
                pair, side = divmod(index, 2)
                row = 2 * first + index
                fresh = values[
                    pair * width : (pair + 1) * width, side * channels : (side + 1) * channels
                ]
                fresh = own_ref[flat(row + RIM_USED + skip, 1, width), :] + fresh
                if hour == 0:
                    fresh = fresh + noise_level * noise_ref[row].astype(f32)
                    own_ref[flat(row, 1, width), :] = mask(fresh, row - rim + RIM_USED)
                else:
                    out_ref[:, row * cols : (row + 1) * cols] = fresh[pad : pad + cols].T.astype(bf16)


def denoise(rows, cols, totals, variables, conds, place, pick, parts, strips, weights):
    mid0, _, _, _, left, _ = parts
    width, channels = cols + 2 * left.shape[1], mid0.shape[2]
    tall = rows + 2 * RIM
    most = (tall - 2) // 2
    points = LANES // PACKED * pick.shape[0] * STRIP
    bf16, f32 = jnp.bfloat16, jnp.float32
    return pl.pallas_call(
        functools.partial(denoise_kernel, rows, cols, totals, variables, conds, width),
        out_shape=jax.ShapeDtypeStruct((channels, rows * cols), bf16),
        in_specs=[pl.BlockSpec(memory_space=pltpu.SMEM)] * 2
        + [pl.BlockSpec(memory_space=pltpu.VMEM)] * 7
        + [pl.BlockSpec(memory_space=pl.ANY)] * len(weights),
        scratch_shapes=[pltpu.VMEM(array.shape, array.dtype) for array in weights]
        + [
            pltpu.SemaphoreType.DMA((len(weights),)),
            pltpu.VMEM((tall, width, channels), bf16),
            pltpu.VMEM((tall - 2 * RIM_USED, width, channels), bf16),
            pltpu.VMEM((tall * width, points), bf16),
            pltpu.VMEM((tall * width, channels), f32),
            pltpu.VMEM((3, tall * width, channels), bf16),
            pltpu.VMEM((most * width, 2 * channels), bf16),
            pltpu.VMEM((3, most * width // 2, channels), bf16),
            pltpu.VMEM((3, tall * width, channels), bf16),
            pltpu.VMEM((most, width, channels), f32),
            pltpu.VMEM((most, width, channels), f32),
            pltpu.VMEM((2, points, channels), bf16),
        ],
        compiler_params=pltpu.CompilerParams(vmem_limit_bytes=VMEM),
        cost_estimate=pl.CostEstimate(flops=10**6, bytes_accessed=10**5, transcendentals=0),
        name="denoise",
    )(place, pick, *parts, strips, *weights)


def conv_weight(weight, depth, width):
    out, _, given = weight.shape
    weight = jnp.pad(weight, ((0, width - out), (0, 0), (0, depth - given)))
    return jnp.transpose(weight, (1, 2, 0)).reshape(9 * depth, width)


def pair_weight(weight):
    row = weight.shape[0] // 3
    return jnp.concatenate(
        [jnp.pad(weight, ((0, row), (0, 0))), jnp.pad(weight, ((row, 0), (0, 0)))], axis=1
    )


def shards(
    global_state,
    spec_filter,
    w_skip,
    w_mix,
    w_decode,
    regional_state,
    noise_draws,
    w_first,
    w_down,
    w_up,
    w_bridge,
    w_last,
    box_lat0,
    box_lon0,
    stencil_lat,
    stencil_lon,
):
    hours = noise_draws.shape[0]
    rows_here, cols_here = regional_state.shape[1:]
    row_start = lax.axis_index(PLANE) * rows_here
    col_start = lax.axis_index("col") * cols_here
    total_rows = rows_here * lax.axis_size(PLANE)
    total_cols = cols_here * lax.axis_size("col")
    assert hours == 2

    variables = regional_state.shape[0]
    conds = w_decode.shape[1]
    lanes = variables + conds
    noisy = (
        regional_state.astype(jnp.float32) + noise_level * noise_draws[0].astype(jnp.float32)
    ).astype(jnp.bfloat16)
    lat_shift = stencil_lat - (row_start + jnp.arange(rows_here, dtype=jnp.int32))[:, None] // RATIO
    lon_shift = stencil_lon - (col_start + jnp.arange(cols_here, dtype=jnp.int32))[None, :] // RATIO
    cells = (rows_here, cols_here)
    mids = jnp.concatenate(
        [
            noisy,
            jnp.zeros((conds,) + cells, jnp.bfloat16),
            lat_shift.astype(jnp.bfloat16)[None],
            lon_shift.astype(jnp.bfloat16)[None],
            jnp.zeros((LANES - lanes - 2,) + cells, jnp.bfloat16),
            noise_draws[1],
            jnp.zeros((LANES - variables,) + cells, jnp.bfloat16),
        ],
        axis=0,
    )
    mids = jnp.transpose(mids.reshape((2, LANES) + cells), (0, 2, 3, 1))
    mid0, mid1 = mids[0], mids[1]
    inner = RIM - RIM_USED
    high = window_extent(rows_here)
    place = jnp.stack([row_start, col_start]).astype(jnp.int32)
    totals = (total_rows, total_cols)

    def prepare():
        lows = jnp.concatenate([mid0[rows_here - RIM :], mid1[rows_here - inner :]], axis=0)
        highs = jnp.concatenate([mid0[:RIM], mid1[:inner]], axis=0)
        above, below = next_to(lows, highs, PLANE)

        def rim_cols(first, first_inner):
            wide, thin = slice(first, first + RIM), slice(first_inner, first_inner + inner)
            noise = jnp.concatenate([above[RIM:, thin], mid1[:, thin], below[RIM:, thin]], axis=0)
            noise = jnp.pad(
                noise, ((RIM_USED, RIM_USED), (0, RIM_COLS - RIM - inner), (0, 0))
            )
            return jnp.concatenate(
                [
                    jnp.concatenate([above[:RIM, wide], mid0[:, wide], below[:RIM, wide]], axis=0),
                    noise,
                ],
                axis=1,
            )

        left, right = next_to(
            rim_cols(cols_here - RIM, cols_here - inner), rim_cols(0, 0), "col"
        )
        weights = (
            pair_weight(conv_weight(0.5 * w_first, LANES, w_first.shape[0])),
            conv_weight(0.125 * w_down, w_down.shape[2], w_down.shape[0]),
            0.5 * w_up.T,
            0.5
            * jnp.concatenate(
                [jnp.pad(w_bridge.T, ((0, 0), (0, LANES))), jnp.pad(w_bridge.T, ((0, 0), (LANES, 0)))],
                axis=0,
            ),
            pair_weight(conv_weight(w_last, w_last.shape[2], LANES)),
        )
        return (mid0, mid1, above, below, left, right), weights

    by_latitude = lax.axis_size("col") == 4 and global_state.shape[0] % 4 == 0
    global_steps = global_by_latitude if by_latitude else global_by_channel
    finish, strips, pick, (parts, weights) = global_steps(
        hours, global_state, spec_filter, w_skip, w_mix, w_decode, box_lat0, box_lon0,
        rows_here, cols_here, prepare,
    )
    regional_final = denoise(
        rows_here, cols_here, totals, variables, conds, place, pick, parts, strips, weights
    )
    regional_final = regional_final[:variables].reshape((variables, rows_here, cols_here))
    return finish(regional_final)


def solution(mesh):
    return jax.shard_map(
        shards,
        mesh=mesh,
        in_specs=(
            P(PLANE, "col", None),
            P(None, None, "col"),
            P(),
            P(),
            P(),
            P(None, PLANE, "col"),
            P(None, None, PLANE, "col"),
            P(),
            P(),
            P(),
            P(),
            P(),
            P(),
            P(),
            P(PLANE, "col"),
            P(PLANE, "col"),
        ),
        out_specs=(P(PLANE, "col", None), P(None, PLANE, "col")),
        check_vma=False,
    )
```

profile of v0, /device:TPU:8, one launch (start us, length us, event | category | flops | bytes accessed | tf_op | source)
XLA Modules:
  0.0 147.0 jit_solution(15476297849299207474)
XLA Ops:
  0.7 1.5 %copy.28 = bf16[2,720,96]{1,0,2:T(2,128)(2,1)S(1)} copy(f32[2,720,96]{1,2,0:T(8,128)} %param.21) | data formatting | bytes 829440 | tf_op args[1]
  2.6 3.1 %constant_dynamic-slice_fusion.2 = (bf16[2,360,384]{2,1,0:T(8,128)(2,1)}, bf16[2,360,384]{2,1,0:T(8,128)(2,1)}, bf16[2,360,384]{2,1,0:T(8,128)(2,1)}, bf16[2,360,384]{2,1,0:T(8,128)(2,1)}) fusion(bf16[8,360,384]{2,1,0:T(8,128)(2,1)} %param.20, s32[]{:T(128)S(6)} %select_n.132, s32[]{:T(128)S(6)} %select_n.130, s32[]{:T(128)S(6)} %select_n.129, s32[]{:T(128)S(6)} %select_n.131), kind=kLoop, calls=%fused_computation.67 | loop fusion | bytes 4423696 | tf_op jit(solution)/shard_map/dynamic_slice | solution.py:349
  5.7 3.0 %collective-permute-start.4 = (bf16[180,96]{0,1:T(8,128)(2,1)S(1)}, bf16[180,96]{0,1:T(8,128)(2,1)}, u32[]{:S(2)}, u32[]{:S(2)}) collective-permute-start(bf16[180,96]{0,1:T(8,128)(2,1)S(1)} %dynamic-slice_convert_fusion), channel_id=1, source_target_pairs={{0,2},{1,3},{2,0},{3,1},{4,6},{5,7},{6,4},{7,5},{8,10},{9,11},{10,... | collective-permute-start | bytes 103688 | tf_op jit(solution)/shard_map/ppermute | solution.py:302
  8.7 2.5 %collective-permute-start.5 = (bf16[180,96]{0,1:T(8,128)(2,1)S(1)}, bf16[180,96]{0,1:T(8,128)(2,1)}, u32[]{:S(2)}, u32[]{:S(2)}) collective-permute-start(bf16[180,96]{0,1:T(8,128)(2,1)S(1)} %dynamic-slice_convert_fusion), channel_id=1, source_target_pairs={{0,1},{1,2},{2,3},{3,0},{4,5},{5,6},{6,7},{7,4},{8,9},{9,10},{10,1... | collective-permute-start | bytes 103688 | tf_op jit(solution)/shard_map/ppermute | solution.py:302
  11.2 1.5 collective-permute-start.1
  17.6 1.1 multiply_bitcast_fusion
  21.0 1.3 fusion.5
  23.9 1.1 copy.30
  25.8 2.4 %collective-permute-start.2 = (bf16[2,360,384]{2,1,0:T(8,128)(2,1)}, bf16[2,360,384]{2,1,0:T(8,128)(2,1)S(1)}, u32[]{:S(2)}, u32[]{:S(2)}) collective-permute-start(bf16[2,360,384]{2,1,0:T(8,128)(2,1)} %get-tuple-element.41), channel_id=1, source_target_pairs={{0,1},{1,2},{2,3},{3,0},{4,5},{5,6},{6,7},{7,4},{8,9},{9,10},{10,1... | collective-permute-start | bytes 1658888 | tf_op jit(solution)/shard_map/ppermute | solution.py:302
  29.0 3.4 %collective-permute-start.6 = (bf16[14,128,128]{2,1,0:T(8,128)(2,1)}, bf16[14,128,128]{2,1,0:T(8,128)(2,1)S(1)}, u32[]{:S(2)}, u32[]{:S(2)}) collective-permute-start(bf16[14,128,128]{2,1,0:T(8,128)(2,1)} %pad_maximum_fusion), channel_id=1, source_target_pairs={{0,4},{4,8},{8,12},{12,16},{16,20},{20,24},{24,28},{1,5},{5,9},{9,... | collective-permute-start | bytes 1376264 | tf_op jit(solution)/shard_map/ppermute | solution.py:422
  33.2 2.5 %collective-permute-done.5 = bf16[180,96]{0,1:T(8,128)(2,1)} collective-permute-done((bf16[180,96]{0,1:T(8,128)(2,1)S(1)}, bf16[180,96]{0,1:T(8,128)(2,1)}, u32[]{:S(2)}, u32[]{:S(2)}) %collective-permute-start.5) | collective-permute-done | bytes 34592 | tf_op jit(solution)/shard_map/ppermute | solution.py:302
  35.7 1.3 collective-permute-start.7
  39.5 1.1 broadcast_in_dim.14
  40.6 5.0 %all-to-all-start = ((bf16[8,180,384]{2,1,0:T(8,128)(2,1)}), bf16[8,180,384]{2,1,0:T(8,128)(2,1)S(1)}, u32[]{:S(2)}, u32[]{:S(2)}) async-start(bf16[8,180,384]{2,1,0:T(8,128)(2,1)} %broadcast_in_dim.14), calls=%async_computation | async-start | bytes 2260992 | tf_op jit(solution)/shard_map/all_to_all | solution.py:87
  45.6 9.7 %collective-permute-done.7.below_ref = bf16[14,128,128]{2,1,0:T(8,128)(2,1)S(1)} collective-permute-done((bf16[14,128,128]{2,1,0:T(8,128)(2,1)S(1)}, bf16[14,128,128]{2,1,0:T(8,128)(2,1)S(1)}, u32[]{:S(2)}, u32[]{:S(2)}) %collective-permute-start.7) | collective-permute-done | bytes 458784 | tf_op jit(solution)/shard_map/ppermute | solution.py:422
  55.5 1.9 %collective-permute-start.8 = (bf16[34,16,128]{2,1,0:T(8,128)(2,1)S(1)}, bf16[34,16,128]{2,1,0:T(8,128)(2,1)S(1)}, u32[]{:S(2)}, u32[]{:S(2)}) collective-permute-start(bf16[34,16,128]{2,1,0:T(8,128)(2,1)S(1)} %pad_maximum_fusion.2), channel_id=1, source_target_pairs={{0,1},{1,2},{2,3},{4,5},{5,6},{6,7},{8,9},{9,10},{10,11},{12,13},{... | collective-permute-start | bytes 417800 | tf_op jit(solution)/shard_map/ppermute | solution.py:422
  57.5 3.9 %collective-permute-start.9 = (bf16[34,16,128]{2,1,0:T(8,128)(2,1)S(1)}, bf16[34,16,128]{2,1,0:T(8,128)(2,1)S(1)}, u32[]{:S(2)}, u32[]{:S(2)}) collective-permute-start(bf16[34,16,128]{2,1,0:T(8,128)(2,1)S(1)} %pad_maximum_fusion.3), channel_id=1, source_target_pairs={{1,0},{2,1},{3,2},{5,4},{6,5},{7,6},{9,8},{10,9},{11,10},{13,12},{... | collective-permute-start | bytes 417800 | tf_op jit(solution)/shard_map/ppermute | solution.py:422
  61.5 1.2 reshape.119.refs_6_
  62.7 21.1 %advance_latitudes.1 = (bf16[2,360,384]{2,1,0:T(8,128)(2,1)}, bf16[2,360,384]{2,1,0:T(8,128)(2,1)}, bf16[2,360,384]{2,1,0:T(8,128)(2,1)}, bf16[2,360,384]{2,1,0:T(8,128)(2,1)}, bf16[4,32,128]{2,1,0:T(8,128)(2,1)}) custom-call(s32[3]{0:T(128)} %pad_add_fusion.1.place_ref, bf16[2,360,384]{2,1,0:T(8,128)(2,1)} %get-tuple-element.42.refs_0_, ...), custom_call_target="tpu_custom_call" | custom-call | flops 32000000000 | bytes 12582912 | tf_op jit(solution)/shard_map/advance_latitudes/pallas_call | solution.py:243
  84.7 2.9 %collective-permute-start.12 = (bf16[32,128]{1,0:T(8,128)(2,1)S(1)}, bf16[32,128]{1,0:T(8,128)(2,1)S(1)}, u32[]{:S(2)}, u32[]{:S(2)}) collective-permute-start(bf16[32,128]{1,0:T(8,128)(2,1)S(1)} %get-tuple-element.97), channel_id=1, source_target_pairs={{0,1},{1,2},{2,3},{3,0},{4,5},{5,6},{6,7},{7,4},{8,9},{9,10},{10,1... | collective-permute-start | bytes 24584 | tf_op jit(solution)/shard_map/ppermute | solution.py:302
  87.6 2.0 %collective-permute-start.11 = (bf16[32,128]{1,0:T(8,128)(2,1)S(1)}, bf16[32,128]{1,0:T(8,128)(2,1)S(1)}, u32[]{:S(2)}, u32[]{:S(2)}) collective-permute-start(bf16[32,128]{1,0:T(8,128)(2,1)S(1)} %get-tuple-element.98), channel_id=1, source_target_pairs={{0,2},{1,3},{2,0},{3,1},{4,6},{5,7},{6,4},{7,5},{8,10},{9,11},{10,... | collective-permute-start | bytes 24584 | tf_op jit(solution)/shard_map/ppermute | solution.py:302
  89.6 2.5 %collective-permute-done.11 = bf16[32,128]{1,0:T(8,128)(2,1)S(1)} collective-permute-done((bf16[32,128]{1,0:T(8,128)(2,1)S(1)}, bf16[32,128]{1,0:T(8,128)(2,1)S(1)}, u32[]{:S(2)}, u32[]{:S(2)}) %collective-permute-start.11) | collective-permute-done | bytes 8224 | tf_op jit(solution)/shard_map/ppermute | solution.py:302
  92.1 1.2 collective-permute-done.10
  93.3 2.8 %collective-permute-start.14 = (bf16[2,360,384]{2,1,0:T(8,128)(2,1)}, bf16[2,360,384]{2,1,0:T(8,128)(2,1)S(1)}, u32[]{:S(2)}, u32[]{:S(2)}) collective-permute-start(bf16[2,360,384]{2,1,0:T(8,128)(2,1)} %get-tuple-element.55), channel_id=1, source_target_pairs={{0,2},{1,3},{2,0},{3,1},{4,6},{5,7},{6,4},{7,5},{8,10},{9,11},{10,... | collective-permute-start | bytes 1658888 | tf_op jit(solution)/shard_map/ppermute | solution.py:302
  96.2 1.9 %collective-permute-start.15 = (bf16[2,360,384]{2,1,0:T(8,128)(2,1)}, bf16[2,360,384]{2,1,0:T(8,128)(2,1)S(1)}, u32[]{:S(2)}, u32[]{:S(2)}) collective-permute-start(bf16[2,360,384]{2,1,0:T(8,128)(2,1)} %get-tuple-element.56), channel_id=1, source_target_pairs={{0,3},{1,0},{2,1},{3,2},{4,7},{5,4},{6,5},{7,6},{8,11},{9,8},{10,9... | collective-permute-start | bytes 1658888 | tf_op jit(solution)/shard_map/ppermute | solution.py:302
  99.5 3.5 %all-to-all-start.1 = ((bf16[8,4,32,128]{3,2,1,0:T(8,128)(2,1)}), bf16[8,4,32,128]{3,2,1,0:T(8,128)(2,1)S(1)}, u32[]{:S(2)}, u32[]{:S(2)}) async-start(bf16[8,4,32,128]{3,2,1,0:T(8,128)(2,1)} %broadcast_in_dim.35), calls=%async_computation.1 | async-start | bytes 524288 | tf_op jit(solution)/shard_map/all_to_all | solution.py:87
  104.8 4.8 %all-to-all-done.1 = bf16[8,4,32,128]{3,2,1,0:T(8,128)(2,1)S(1)} async-done(((bf16[8,4,32,128]{3,2,1,0:T(8,128)(2,1)}), bf16[8,4,32,128]{3,2,1,0:T(8,128)(2,1)S(1)}, u32[]{:S(2)}, u32[]{:S(2)}) %all-to-all-start.1) | async-done | bytes 262176 | tf_op jit(solution)/shard_map/all_to_all | solution.py:87
  110.3 17.7 %denoise.1 = bf16[128,2048]{1,0:T(8,128)(2,1)} custom-call(s32[2]{0:T(128)} %pad_add_fusion.2.place_ref, s32[8]{0:T(128)} %fusion.19.pick_ref, bf16[16,128,128]{2,1,0:T(8,128)(2,1)} %copy-done, bf16[16,128,128]{2,1,0:T(8,128)(2,1)} %copy-done.1, bf16[14,128,128]{2,1,0:T(8,128)(2,1)} %copy-done.4, bf16[14,128,128]{2,1,0:T(8,128)(2,1)} %copy-done.5, ...), custom_call_target="tpu_custom_call" | custom-call | flops 1000000 | bytes 100000 | tf_op jit(solution)/shard_map/denoise/pallas_call | solution.py:629
  128.0 1.0 slice.122
  130.4 9.6 %collective-permute-done.14.refs_2_ = bf16[2,360,384]{2,1,0:T(8,128)(2,1)S(1)} collective-permute-done((bf16[2,360,384]{2,1,0:T(8,128)(2,1)}, bf16[2,360,384]{2,1,0:T(8,128)(2,1)S(1)}, u32[]{:S(2)}, u32[]{:S(2)}) %collective-permute-start.14) | collective-permute-done | bytes 552992 | tf_op jit(solution)/shard_map/ppermute | solution.py:302
  140.0 3.1 %collective-permute-done.15.refs_3_ = bf16[2,360,384]{2,1,0:T(8,128)(2,1)S(1)} collective-permute-done((bf16[2,360,384]{2,1,0:T(8,128)(2,1)}, bf16[2,360,384]{2,1,0:T(8,128)(2,1)S(1)}, u32[]{:S(2)}, u32[]{:S(2)}) %collective-permute-start.15) | collective-permute-done | bytes 552992 | tf_op jit(solution)/shard_map/ppermute | solution.py:302
  143.9 2.9 %collate.1 = bf16[8,360,384]{2,1,0:T(8,128)(2,1)} custom-call(s32[4]{0:T(128)} %pad_add_fusion.place_ref, bf16[2,360,384]{2,1,0:T(8,128)(2,1)} %get-tuple-element.69.refs_0_, bf16[2,360,384]{2,1,0:T(8,128)(2,1)} %copy-done.7, bf16[2,360,384]{2,1,0:T(8,128)(2,1)} %copy-done.8, bf16[2,360,384]{2,1,0:T(8,128)(2,1)} %copy-done.9), custom_call_target="tpu_custom_call" | custom-call | tf_op jit(solution)/shard_map/collate/pallas_call | solution.py:289
  (119 shorter events, 19.7 us)
Async XLA Ops:
  2.6 11.4 %copy-start.3 = (bf16[2,99,16,128]{3,2,1,0:T(8,128)(2,1)S(1)}, bf16[2,99,16,128]{3,2,1,0:T(8,128)(2,1)}, u32[]{:S(2)}) copy-start(bf16[2,99,16,128]{3,2,1,0:T(8,128)(2,1)} %param.26) | copy-start | bytes 2433028
  2.6 11.4 %copy-start.10 = (bf16[99,16,128]{2,1,0:T(8,128)(2,1)S(1)}, bf16[99,16,128]{2,1,0:T(8,128)(2,1)}, u32[]{:S(2)}) copy-start(bf16[99,16,128]{2,1,0:T(8,128)(2,1)} %param.25) | copy-start | bytes 1216516
  2.6 11.6 %copy-start.21 = (s32[16,128]{1,0:T(8,128)S(1)}, s32[16,128]{1,0:T(8,128)}, u32[]{:S(2)}) copy-start(s32[16,128]{1,0:T(8,128)} %param.34) | copy-start | bytes 24580
  2.6 11.7 %copy-start.22 = (s32[16,128]{1,0:T(8,128)S(1)}, s32[16,128]{1,0:T(8,128)}, u32[]{:S(2)}) copy-start(s32[16,128]{1,0:T(8,128)} %param.35) | copy-start | bytes 24580
  5.7 20.1 %collective-permute-start.3 = (bf16[180,96]{0,1:T(8,128)(2,1)S(1)}, bf16[180,96]{0,1:T(8,128)(2,1)}, u32[]{:S(2)}, u32[]{:S(2)}) collective-permute-start(bf16[180,96]{0,1:T(8,128)(2,1)S(1)} %dynamic-slice_convert_fusion), channel_id=1, source_target_pairs={{0,3},{1,0},{2,1},{3,2},{4,7},{5,4},{6,5},{7,6},{8,11},{9,8},{10,9... | collective-permute-start | bytes 103688 | tf_op jit(solution)/shard_map/ppermute | solution.py:302
  5.7 23.3 %collective-permute-start.4 = (bf16[180,96]{0,1:T(8,128)(2,1)S(1)}, bf16[180,96]{0,1:T(8,128)(2,1)}, u32[]{:S(2)}, u32[]{:S(2)}) collective-permute-start(bf16[180,96]{0,1:T(8,128)(2,1)S(1)} %dynamic-slice_convert_fusion), channel_id=1, source_target_pairs={{0,2},{1,3},{2,0},{3,1},{4,6},{5,7},{6,4},{7,5},{8,10},{9,11},{10,... | collective-permute-start | bytes 103688 | tf_op jit(solution)/shard_map/ppermute | solution.py:302
  8.7 26.9 %collective-permute-start.5 = (bf16[180,96]{0,1:T(8,128)(2,1)S(1)}, bf16[180,96]{0,1:T(8,128)(2,1)}, u32[]{:S(2)}, u32[]{:S(2)}) collective-permute-start(bf16[180,96]{0,1:T(8,128)(2,1)S(1)} %dynamic-slice_convert_fusion), channel_id=1, source_target_pairs={{0,1},{1,2},{2,3},{3,0},{4,5},{5,6},{6,7},{7,4},{8,9},{9,10},{10,1... | collective-permute-start | bytes 103688 | tf_op jit(solution)/shard_map/ppermute | solution.py:302
  11.2 50.3 %collective-permute-start = (bf16[2,360,384]{2,1,0:T(8,128)(2,1)}, bf16[2,360,384]{2,1,0:T(8,128)(2,1)}, u32[]{:S(2)}, u32[]{:S(2)}) collective-permute-start(bf16[2,360,384]{2,1,0:T(8,128)(2,1)} %get-tuple-element.39), channel_id=1, source_target_pairs={{0,3},{1,0},{2,1},{3,2},{4,7},{5,4},{6,5},{7,6},{8,11},{9,8},{10,9... | collective-permute-start | bytes 1658888 | tf_op jit(solution)/shard_map/ppermute | solution.py:302
  11.2 50.3 %collective-permute-start.1 = (bf16[2,360,384]{2,1,0:T(8,128)(2,1)}, bf16[2,360,384]{2,1,0:T(8,128)(2,1)}, u32[]{:S(2)}, u32[]{:S(2)}) collective-permute-start(bf16[2,360,384]{2,1,0:T(8,128)(2,1)} %get-tuple-element.40), channel_id=1, source_target_pairs={{0,2},{1,3},{2,0},{3,1},{4,6},{5,7},{6,4},{7,5},{8,10},{9,11},{10,... | collective-permute-start | bytes 1658888 | tf_op jit(solution)/shard_map/ppermute | solution.py:302
  15.6 4.8 %copy-start.1 = (bf16[16,128,128]{2,1,0:T(8,128)(2,1)}, bf16[16,128,128]{2,1,0:T(8,128)(2,1)S(1)}, u32[]{:S(2)}) copy-start(bf16[16,128,128]{2,1,0:T(8,128)(2,1)S(1)} %get-tuple-element.58.mid1_ref) | copy-start | bytes 1572868
  15.6 5.4 %copy-start = (bf16[16,128,128]{2,1,0:T(8,128)(2,1)}, bf16[16,128,128]{2,1,0:T(8,128)(2,1)S(1)}, u32[]{:S(2)}) copy-start(bf16[16,128,128]{2,1,0:T(8,128)(2,1)S(1)} %get-tuple-element.57.mid0_ref) | copy-start | bytes 1572868
  22.4 5.8 %copy-start.13 = (bf16[180,672]{0,1:T(8,128)(2,1)S(1)}, bf16[180,672]{0,1:T(8,128)(2,1)}, u32[]{:S(2)}) copy-start(bf16[180,672]{0,1:T(8,128)(2,1)} %constant_dynamic-update-slice_fusion.6) | copy-start | bytes 725764
  25.8 35.7 %collective-permute-start.2 = (bf16[2,360,384]{2,1,0:T(8,128)(2,1)}, bf16[2,360,384]{2,1,0:T(8,128)(2,1)S(1)}, u32[]{:S(2)}, u32[]{:S(2)}) collective-permute-start(bf16[2,360,384]{2,1,0:T(8,128)(2,1)} %get-tuple-element.41), channel_id=1, source_target_pairs={{0,1},{1,2},{2,3},{3,0},{4,5},{5,6},{6,7},{7,4},{8,9},{9,10},{10,1... | collective-permute-start | bytes 1658888 | tf_op jit(solution)/shard_map/ppermute | solution.py:302
  29.0 26.4 %collective-permute-start.6 = (bf16[14,128,128]{2,1,0:T(8,128)(2,1)}, bf16[14,128,128]{2,1,0:T(8,128)(2,1)S(1)}, u32[]{:S(2)}, u32[]{:S(2)}) collective-permute-start(bf16[14,128,128]{2,1,0:T(8,128)(2,1)} %pad_maximum_fusion), channel_id=1, source_target_pairs={{0,4},{4,8},{8,12},{12,16},{16,20},{20,24},{24,28},{1,5},{5,9},{9,... | collective-permute-start | bytes 1376264 | tf_op jit(solution)/shard_map/ppermute | solution.py:422
  35.7 19.7 %collective-permute-start.7 = (bf16[14,128,128]{2,1,0:T(8,128)(2,1)S(1)}, bf16[14,128,128]{2,1,0:T(8,128)(2,1)S(1)}, u32[]{:S(2)}, u32[]{:S(2)}) collective-permute-start(bf16[14,128,128]{2,1,0:T(8,128)(2,1)S(1)} %pad_maximum_fusion.1), channel_id=1, source_target_pairs={{4,0},{8,4},{12,8},{16,12},{20,16},{24,20},{28,24},{5,1},{9,5},{13... | collective-permute-start | bytes 1376264 | tf_op jit(solution)/shard_map/ppermute | solution.py:422
  39.5 15.8 %copy-start.17 = (bf16[16,5,128]{2,1,0:T(8,128)(2,1)S(1)}, bf16[16,5,128]{2,1,0:T(8,128)(2,1)}, u32[]{:S(2)}) copy-start(bf16[16,5,128]{2,1,0:T(8,128)(2,1)} %get-tuple-element.87) | copy-start | bytes 61444
  40.6 16.8 %copy-start.16 = (bf16[16,5,128]{2,1,0:T(8,128)(2,1)S(1)}, bf16[16,5,128]{2,1,0:T(8,128)(2,1)}, u32[]{:S(2)}) copy-start(bf16[16,5,128]{2,1,0:T(8,128)(2,1)} %get-tuple-element.86) | copy-start | bytes 61444
  40.6 20.9 %all-to-all-start = ((bf16[8,180,384]{2,1,0:T(8,128)(2,1)}), bf16[8,180,384]{2,1,0:T(8,128)(2,1)S(1)}, u32[]{:S(2)}, u32[]{:S(2)}) async-start(bf16[8,180,384]{2,1,0:T(8,128)(2,1)} %broadcast_in_dim.14), calls=%async_computation | async-start | bytes 2260992 | tf_op jit(solution)/shard_map/all_to_all | solution.py:87
  55.3 7.4 %copy-start.5 = (bf16[14,128,128]{2,1,0:T(8,128)(2,1)}, bf16[14,128,128]{2,1,0:T(8,128)(2,1)S(1)}, u32[]{:S(2)}) copy-start(bf16[14,128,128]{2,1,0:T(8,128)(2,1)S(1)} %collective-permute-done.7.below_ref) | copy-start | bytes 1376260
  55.3 7.4 %copy-start.4 = (bf16[14,128,128]{2,1,0:T(8,128)(2,1)}, bf16[14,128,128]{2,1,0:T(8,128)(2,1)S(1)}, u32[]{:S(2)}) copy-start(bf16[14,128,128]{2,1,0:T(8,128)(2,1)S(1)} %collective-permute-done.6.above_ref) | copy-start | bytes 1376260
  55.5 28.3 %collective-permute-start.8 = (bf16[34,16,128]{2,1,0:T(8,128)(2,1)S(1)}, bf16[34,16,128]{2,1,0:T(8,128)(2,1)S(1)}, u32[]{:S(2)}, u32[]{:S(2)}) collective-permute-start(bf16[34,16,128]{2,1,0:T(8,128)(2,1)S(1)} %pad_maximum_fusion.2), channel_id=1, source_target_pairs={{0,1},{1,2},{2,3},{4,5},{5,6},{6,7},{8,9},{9,10},{10,11},{12,13},{... | collective-permute-start | bytes 417800 | tf_op jit(solution)/shard_map/ppermute | solution.py:422
  57.5 26.3 %collective-permute-start.9 = (bf16[34,16,128]{2,1,0:T(8,128)(2,1)S(1)}, bf16[34,16,128]{2,1,0:T(8,128)(2,1)S(1)}, u32[]{:S(2)}, u32[]{:S(2)}) collective-permute-start(bf16[34,16,128]{2,1,0:T(8,128)(2,1)S(1)} %pad_maximum_fusion.3), channel_id=1, source_target_pairs={{1,0},{2,1},{3,2},{5,4},{6,5},{7,6},{9,8},{10,9},{11,10},{13,12},{... | collective-permute-start | bytes 417800 | tf_op jit(solution)/shard_map/ppermute | solution.py:422
  83.8 25.8 %copy-start.14 = (bf16[34,16,128]{2,1,0:T(8,128)(2,1)}, bf16[34,16,128]{2,1,0:T(8,128)(2,1)S(1)}, u32[]{:S(2)}) copy-start(bf16[34,16,128]{2,1,0:T(8,128)(2,1)S(1)} %collective-permute-done.8.left_ref) | copy-start | bytes 417796
  83.8 25.7 %copy-start.15 = (bf16[34,16,128]{2,1,0:T(8,128)(2,1)}, bf16[34,16,128]{2,1,0:T(8,128)(2,1)S(1)}, u32[]{:S(2)}) copy-start(bf16[34,16,128]{2,1,0:T(8,128)(2,1)S(1)} %collective-permute-done.9.right_ref) | copy-start | bytes 417796
  84.7 4.9 %collective-permute-start.12 = (bf16[32,128]{1,0:T(8,128)(2,1)S(1)}, bf16[32,128]{1,0:T(8,128)(2,1)S(1)}, u32[]{:S(2)}, u32[]{:S(2)}) collective-permute-start(bf16[32,128]{1,0:T(8,128)(2,1)S(1)} %get-tuple-element.97), channel_id=1, source_target_pairs={{0,1},{1,2},{2,3},{3,0},{4,5},{5,6},{6,7},{7,4},{8,9},{9,10},{10,1... | collective-permute-start | bytes 24584 | tf_op jit(solution)/shard_map/ppermute | solution.py:302
  87.6 4.5 %collective-permute-start.11 = (bf16[32,128]{1,0:T(8,128)(2,1)S(1)}, bf16[32,128]{1,0:T(8,128)(2,1)S(1)}, u32[]{:S(2)}, u32[]{:S(2)}) collective-permute-start(bf16[32,128]{1,0:T(8,128)(2,1)S(1)} %get-tuple-element.98), channel_id=1, source_target_pairs={{0,2},{1,3},{2,0},{3,1},{4,6},{5,7},{6,4},{7,5},{8,10},{9,11},{10,... | collective-permute-start | bytes 24584 | tf_op jit(solution)/shard_map/ppermute | solution.py:302
  89.6 3.7 %collective-permute-start.10 = (bf16[32,128]{1,0:T(8,128)(2,1)S(1)}, bf16[32,128]{1,0:T(8,128)(2,1)S(1)}, u32[]{:S(2)}, u32[]{:S(2)}) collective-permute-start(bf16[32,128]{1,0:T(8,128)(2,1)S(1)} %get-tuple-element.99), channel_id=1, source_target_pairs={{0,3},{1,0},{2,1},{3,2},{4,7},{5,4},{6,5},{7,6},{8,11},{9,8},{10,9... | collective-permute-start | bytes 24584 | tf_op jit(solution)/shard_map/ppermute | solution.py:302
  93.3 37.1 %collective-permute-start.13 = (bf16[2,360,384]{2,1,0:T(8,128)(2,1)}, bf16[2,360,384]{2,1,0:T(8,128)(2,1)S(1)}, u32[]{:S(2)}, u32[]{:S(2)}) collective-permute-start(bf16[2,360,384]{2,1,0:T(8,128)(2,1)} %get-tuple-element.54), channel_id=1, source_target_pairs={{0,1},{1,2},{2,3},{3,0},{4,5},{5,6},{6,7},{7,4},{8,9},{9,10},{10,1... | collective-permute-start | bytes 1658888 | tf_op jit(solution)/shard_map/ppermute | solution.py:302
  93.3 46.7 %collective-permute-start.14 = (bf16[2,360,384]{2,1,0:T(8,128)(2,1)}, bf16[2,360,384]{2,1,0:T(8,128)(2,1)S(1)}, u32[]{:S(2)}, u32[]{:S(2)}) collective-permute-start(bf16[2,360,384]{2,1,0:T(8,128)(2,1)} %get-tuple-element.55), channel_id=1, source_target_pairs={{0,2},{1,3},{2,0},{3,1},{4,6},{5,7},{6,4},{7,5},{8,10},{9,11},{10,... | collective-permute-start | bytes 1658888 | tf_op jit(solution)/shard_map/ppermute | solution.py:302
  96.2 46.9 %collective-permute-start.15 = (bf16[2,360,384]{2,1,0:T(8,128)(2,1)}, bf16[2,360,384]{2,1,0:T(8,128)(2,1)S(1)}, u32[]{:S(2)}, u32[]{:S(2)}) collective-permute-start(bf16[2,360,384]{2,1,0:T(8,128)(2,1)} %get-tuple-element.56), channel_id=1, source_target_pairs={{0,3},{1,0},{2,1},{3,2},{4,7},{5,4},{6,5},{7,6},{8,11},{9,8},{10,9... | collective-permute-start | bytes 1658888 | tf_op jit(solution)/shard_map/ppermute | solution.py:302
  99.5 10.0 %all-to-all-start.1 = ((bf16[8,4,32,128]{3,2,1,0:T(8,128)(2,1)}), bf16[8,4,32,128]{3,2,1,0:T(8,128)(2,1)S(1)}, u32[]{:S(2)}, u32[]{:S(2)}) async-start(bf16[8,4,32,128]{3,2,1,0:T(8,128)(2,1)} %broadcast_in_dim.35), calls=%async_computation.1 | async-start | bytes 524288 | tf_op jit(solution)/shard_map/all_to_all | solution.py:87
  130.4 12.8 %copy-start.7 = (bf16[2,360,384]{2,1,0:T(8,128)(2,1)}, bf16[2,360,384]{2,1,0:T(8,128)(2,1)S(1)}, u32[]{:S(2)}) copy-start(bf16[2,360,384]{2,1,0:T(8,128)(2,1)S(1)} %collective-permute-done.13.refs_1_) | copy-start | bytes 1658884
  (10 other events, 19.1 us)
where the time goes:
time: 149 us; the launch traced here: 147 us
  Pallas kernels  41.8 us (28%)
  starting transfers between devices  38.1 us (26%)
  waiting for transfers between devices  33.8 us (23%)
  local copies, waits for them, and re-layouts  23 us (15%)
  other arithmetic  7.59 us (5%)
  between operations  2.82 us (2%)
    pallas_call x1, Pallas kernels, advance_latitudes(): pl.pallas_call(functools.partial(latitude_kernel, hours, turns, step), ou...  21.1 us
    ppermute x12, waiting for transfers between devices, shift(): lax.ppermute(block, axis, [(source, (source + step) % count) for source i...  19.3 us
    ppermute x12, starting transfers between devices, shift(): lax.ppermute(block, axis, [(source, (source + step) % count) for source i...  19.1 us
    pallas_call x1, Pallas kernels, denoise(): pl.pallas_call(functools.partial(denoise_kernel, rows, cols, totals, vari...  17.7 us
    ppermute x2, waiting for transfers between devices, next_to(): lax.ppermute(high, axis, backward)  9.69 us
    all_to_all x2, starting transfers between devices, exchange(): return lax.all_to_all(blocks, axis, split_axis=0, concat_axis=0, tiled=True)  8.46 us
    unnamed x62, local copies, waits for them, and re-layouts  8.07 us
    ppermute x2, starting transfers between devices, next_to(): lax.ppermute(low, axis, forward)  5.33 us
  transfers between devices with their start and end apart: 18, of which 8 were waited for; matrix products, arithmetic and copies ran while one was open for 15% of the time, Pallas kernels for 26%

commit v1 on v0

--- a/solution.py
+++ b/solution.py
@@ -153,17 +153,12 @@
         tiles = [gain_ref[index, rows, :] for index in range(channels // LANES)]
         return jnp.concatenate(tiles * turns, axis=1)
 
-    def gain(spectrum, low, stride):
-        half = spectrum.shape[0] // 2
-        real, imag = spectrum[:half], spectrum[half:]
-        gain_real = gain_rows(low, half, stride)
-        gain_imag = gain_rows(modes + low, half, stride)
-        return jnp.concatenate(
-            [
-                (real * gain_real - imag * gain_imag).astype(bf16),
-                (real * gain_imag + imag * gain_real).astype(bf16),
-            ],
-            axis=0,
+    def gain(real, imag, low, stride):
+        gain_real = gain_rows(low, real.shape[0], stride)
+        gain_imag = gain_rows(modes + low, real.shape[0], stride)
+        return (
+            (real * gain_real - imag * gain_imag).astype(bf16),
+            (real * gain_imag + imag * gain_real).astype(bf16),
         )
 
     def dot(left, right):
@@ -173,33 +168,57 @@
         pieces = [
             state_ref[index * padded : (index + 1) * padded, :].astype(f32) for index in range(4)
         ]
-        both, other = pieces[0] + pieces[2], pieces[1] + pieces[3]
-        spectra = [
-            dot(even_forward_ref[index], mixed.astype(bf16))
-            for index, mixed in enumerate((both + other, both - other))
-        ]
-        mixed = jnp.concatenate([pieces[0] - pieces[2], pieces[1] - pieces[3]], axis=0)
-        spectra.append(dot(odd_forward_ref[...], mixed.astype(bf16)))
+        mixed = jnp.concatenate([pieces[0] - pieces[2], pieces[1] - pieces[3]], axis=0).astype(bf16)
+        span_odd = odd_forward_ref.shape[0] // 2
+        thirds = span_odd // 3
+        spectra = []
+        for index in range(3):
+            low = index * thirds
+            spectra.append(
+                (
+                    dot(odd_forward_ref[low : low + thirds, :], mixed),
+                    dot(odd_forward_ref[span_odd + low : span_odd + low + thirds, :], mixed),
+                )
+            )
+            if index == 0:
+                both, other = pieces[0] + pieces[2], pieces[1] + pieces[3]
+                mixes = [(both + other).astype(bf16), (both - other).astype(bf16)]
+        evens = [dot(even_forward_ref[index], mixes[index]) for index in range(2)]
         if hour == 0:
             copies[0].wait()
             spread_gains()
             for copy in copies[1:]:
                 copy.wait()
-        shares = [
-            dot(even_inverse_ref[index], gain(spectra[index], 2 * index, 4)) for index in range(2)
-        ]
-        odd = dot(odd_inverse_ref[...], gain(spectra[2], 1, 2))
-        for index in range(4):
-            here = slice(index * padded, (index + 1) * padded)
-            even = shares[0] + shares[1] if index % 2 == 0 else shares[0] - shares[1]
-            part = odd[:padded] if index % 2 == 0 else odd[padded:]
-            spectral = even + part if index < 2 else even - part
-            for turn in range(turns):
-                lanes = slice(turn * channels, (turn + 1) * channels)
-                state = state_ref[here, lanes]
-                activated = gelu(spectral[:, lanes] + dot(state, skip_ref[...])).astype(bf16)
-                update = dot(activated, mix_ref[...])
-                state_ref[here, lanes] = (state.astype(f32) + update).astype(bf16)
+        odd = [gain(*spectra[index], 1 + 2 * index * thirds, 2) for index in range(3)]
+        odd = jnp.concatenate([part[0] for part in odd] + [part[1] for part in odd], axis=0)
+        odd_shares = [dot(odd_inverse_ref[:padded, :], odd)]
+        shares = []
+        for index in range(2):
+            half = evens[index].shape[0] // 2
+            even = gain(evens[index][:half], evens[index][half:], 2 * index, 4)
+            shares.append(dot(even_inverse_ref[index], jnp.concatenate(even, axis=0)))
+        odd_shares.append(dot(odd_inverse_ref[padded:, :], odd))
+
+        def block_of(ref, index, turn):
+            return ref[
+                index * padded : (index + 1) * padded, turn * channels : (turn + 1) * channels
+            ]
+
+        order = [(index, turn) for index in (0, 2, 1, 3) for turn in range(turns)]
+        skipped = dot(block_of(state_ref, *order[0]), skip_ref[...])
+        for place, (index, turn) in enumerate(order):
+            if place + 1 < len(order):
+                following = dot(block_of(state_ref, *order[place + 1]), skip_ref[...])
+            if turn == 0:
+                even = shares[0] + shares[1] if index % 2 == 0 else shares[0] - shares[1]
+                spectral = even + odd_shares[index % 2] if index < 2 else even - odd_shares[index % 2]
+            own = spectral[:, turn * channels : (turn + 1) * channels]
+            activated = gelu(own + skipped).astype(bf16)
+            fresh = block_of(state_ref, index, turn).astype(f32) + dot(activated, mix_ref[...])
+            state_ref[
+                index * padded : (index + 1) * padded, turn * channels : (turn + 1) * channels
+            ] = fresh.astype(bf16)
+            skipped = following
 
         for index in range(2):
             here = pl.ds(pl.multiple_of(place_ref[index] * padded, LANES), padded)
@@ -270,17 +289,23 @@
 
 
 def collate_kernel(count, place_ref, *refs):
-    pieces, out_ref, sems = refs[:count], refs[count], refs[count + 1]
-    copies = [
+    far, out_ref, near, sems = refs[:count], refs[count], refs[count + 1 : -1], refs[-1]
+    loads = [
+        pltpu.make_async_copy(far[index], near[index], sems.at[0, index]) for index in range(count)
+    ]
+    stores = [
         pltpu.make_async_copy(
-            piece, out_ref.at[pl.ds(place_ref[index], piece.shape[0])], sems.at[index]
+            near[index], out_ref.at[pl.ds(place_ref[index], near[index].shape[0])], sems.at[1, index]
         )
-        for index, piece in enumerate(pieces)
+        for index in range(count)
     ]
-    for copy in copies:
-        copy.start()
-    for copy in copies:
-        copy.wait()
+    for load in loads:
+        load.start()
+    for load, store in zip(loads, stores):
+        load.wait()
+        store.start()
+    for store in stores:
+        store.wait()
 
 
 def collate(place, pieces):
@@ -290,9 +315,11 @@
         functools.partial(collate_kernel, count),
         out_shape=jax.ShapeDtypeStruct((count * turns, piece, channels), pieces[0].dtype),
         in_specs=[pl.BlockSpec(memory_space=pltpu.SMEM)]
-        + [pl.BlockSpec(memory_space=pltpu.VMEM)] * count,
+        + [pl.BlockSpec(memory_space=pl.ANY)] * count,
         out_specs=pl.BlockSpec(memory_space=pl.ANY),
-        scratch_shapes=[pltpu.SemaphoreType.DMA((count,))],
+        scratch_shapes=[pltpu.VMEM(block.shape, block.dtype) for block in pieces]
+        + [pltpu.SemaphoreType.DMA((2, count))],
+        compiler_params=pltpu.CompilerParams(vmem_limit_bytes=VMEM),
         name="collate",
     )(place, *pieces)
 
@@ -358,13 +385,14 @@
     outcome, strips = advance_latitudes(
         hours, cols_here // RATIO, place, received, tables, gains, w_skip, w_mix, w_decode
     )
-    strips, parts = lax.optimization_barrier((strips, parts))
-    near = []
-    for step in range(count):
-        strip = lax.dynamic_index_in_dim(strips, (me - step) % count, 0, keepdims=False)
-        near.append(shift(strip, "col", -step) if step else strip)
-    near, outcome = lax.optimization_barrier((jnp.stack(near), outcome))
-    got = spread(near, PLANE)
+    near = [
+        lax.dynamic_index_in_dim(strips, (me - step) % count, 0, keepdims=False)
+        for step in range(count)
+    ]
+    near, parts = lax.optimization_barrier((near, parts))
+    near = [shift(strip, "col", -step) if step else strip for step, strip in enumerate(near)]
+    near, outcome = lax.optimization_barrier((near, outcome))
+    got = spread(jnp.stack(near), PLANE)
     plane = lax.axis_size(PLANE)
     got = got.reshape((plane * lats_here, -1, LANES))
     lat = box_lat0[0] - window_base() + lax.axis_index(PLANE) * (rows_here // RATIO)

time: 149 us -> 149 us (level)
    all_to_all x2, starting transfers between devices: 8.46 us -> 10.1 us  [exchange(): return lax.all_to_all(blocks, axis, split_axis=0, concat_axis=0, tiled=True)]
  transfers between devices with their start and end apart: 18 -> 18, of which waited for: 8 -> 7; matrix products, arithmetic and copies ran while one was open for 15% -> 16% of each run, Pallas kernels for 26% -> 26%
where the time goes in v1:
time: 149 us; the launch traced here: 146 us
  Pallas kernels  40.6 us (27%)
  starting transfers between devices  39.2 us (26%)
  waiting for transfers between devices  32.7 us (22%)
  local copies, waits for them, and re-layouts  22.9 us (15%)
  other arithmetic  7.59 us (5%)
  between operations  2.81 us (2%)
    pallas_call x1, Pallas kernels, advance_latitudes(): pl.pallas_call(functools.partial(latitude_kernel, hours, turns, step), ou...  19.8 us
    ppermute x12, starting transfers between devices, shift(): lax.ppermute(block, axis, [(source, (source + step) % count) for source i...  18.6 us
    ppermute x12, waiting for transfers between devices, shift(): lax.ppermute(block, axis, [(source, (source + step) % count) for source i...  18.3 us
    pallas_call x1, Pallas kernels, denoise(): pl.pallas_call(functools.partial(denoise_kernel, rows, cols, totals, vari...  17.7 us
    all_to_all x2, starting transfers between devices, exchange(): return lax.all_to_all(blocks, axis, split_axis=0, concat_axis=0, tiled=True)  10.1 us
    ppermute x2, waiting for transfers between devices, next_to(): lax.ppermute(high, axis, backward)  9.69 us
    unnamed x62, local copies, waits for them, and re-layouts  8.07 us
    ppermute x2, starting transfers between devices, next_to(): lax.ppermute(low, axis, forward)  5.33 us
  transfers between devices with their start and end apart: 18, of which 7 were waited for; matrix products, arithmetic and copies ran while one was open for 16% of the time, Pallas kernels for 26%

profile of v1, /device:TPU:8, one launch (start us, length us, event | category | flops | bytes accessed | tf_op | source)
XLA Modules:
  0.0 145.9 jit_solution(10914478779613876999)
XLA Ops:
  0.7 1.5 %copy.28 = bf16[2,720,96]{1,0,2:T(2,128)(2,1)S(1)} copy(f32[2,720,96]{1,2,0:T(8,128)} %param.21) | data formatting | bytes 829440 | tf_op args[1]
  2.6 3.1 %constant_dynamic-slice_fusion.1 = (bf16[2,360,384]{2,1,0:T(8,128)(2,1)}, bf16[2,360,384]{2,1,0:T(8,128)(2,1)}, bf16[2,360,384]{2,1,0:T(8,128)(2,1)}, bf16[2,360,384]{2,1,0:T(8,128)(2,1)}) fusion(bf16[8,360,384]{2,1,0:T(8,128)(2,1)} %param.20, s32[]{:T(128)S(6)} %select_n.132, s32[]{:T(128)S(6)} %select_n.130, s32[]{:T(128)S(6)} %select_n.129, s32[]{:T(128)S(6)} %select_n.131), kind=kLoop, calls=%fused_computation.67 | loop fusion | bytes 4423696 | tf_op jit(solution)/shard_map/dynamic_slice | solution.py:376
  5.7 3.0 %collective-permute-start.4 = (bf16[180,96]{0,1:T(8,128)(2,1)S(1)}, bf16[180,96]{0,1:T(8,128)(2,1)}, u32[]{:S(2)}, u32[]{:S(2)}) collective-permute-start(bf16[180,96]{0,1:T(8,128)(2,1)S(1)} %dynamic-slice_convert_fusion), channel_id=1, source_target_pairs={{0,2},{1,3},{2,0},{3,1},{4,6},{5,7},{6,4},{7,5},{8,10},{9,11},{10,... | collective-permute-start | bytes 103688 | tf_op jit(solution)/shard_map/ppermute | solution.py:329
  8.7 2.5 %collective-permute-start.5 = (bf16[180,96]{0,1:T(8,128)(2,1)S(1)}, bf16[180,96]{0,1:T(8,128)(2,1)}, u32[]{:S(2)}, u32[]{:S(2)}) collective-permute-start(bf16[180,96]{0,1:T(8,128)(2,1)S(1)} %dynamic-slice_convert_fusion), channel_id=1, source_target_pairs={{0,1},{1,2},{2,3},{3,0},{4,5},{5,6},{6,7},{7,4},{8,9},{9,10},{10,1... | collective-permute-start | bytes 103688 | tf_op jit(solution)/shard_map/ppermute | solution.py:329
  11.2 1.5 %collective-permute-start.1 = (bf16[2,360,384]{2,1,0:T(8,128)(2,1)}, bf16[2,360,384]{2,1,0:T(8,128)(2,1)}, u32[]{:S(2)}, u32[]{:S(2)}) collective-permute-start(bf16[2,360,384]{2,1,0:T(8,128)(2,1)} %get-tuple-element.46), channel_id=1, source_target_pairs={{0,2},{1,3},{2,0},{3,1},{4,6},{5,7},{6,4},{7,5},{8,10},{9,11},{10,... | collective-permute-start | bytes 1658888 | tf_op jit(solution)/shard_map/ppermute | solution.py:329
  14.5 1.0 copy.36
  17.6 1.1 multiply_bitcast_fusion
  21.0 1.3 fusion.5
  23.9 1.1 copy.30
  25.8 2.4 %collective-permute-start.2 = (bf16[2,360,384]{2,1,0:T(8,128)(2,1)}, bf16[2,360,384]{2,1,0:T(8,128)(2,1)S(1)}, u32[]{:S(2)}, u32[]{:S(2)}) collective-permute-start(bf16[2,360,384]{2,1,0:T(8,128)(2,1)} %get-tuple-element.47), channel_id=1, source_target_pairs={{0,1},{1,2},{2,3},{3,0},{4,5},{5,6},{6,7},{7,4},{8,9},{9,10},{10,1... | collective-permute-start | bytes 1658888 | tf_op jit(solution)/shard_map/ppermute | solution.py:329
  29.0 3.4 %collective-permute-start.6 = (bf16[14,128,128]{2,1,0:T(8,128)(2,1)}, bf16[14,128,128]{2,1,0:T(8,128)(2,1)S(1)}, u32[]{:S(2)}, u32[]{:S(2)}) collective-permute-start(bf16[14,128,128]{2,1,0:T(8,128)(2,1)} %pad_maximum_fusion), channel_id=1, source_target_pairs={{0,4},{4,8},{8,12},{12,16},{16,20},{20,24},{24,28},{1,5},{5,9},{9,... | collective-permute-start | bytes 1376264 | tf_op jit(solution)/shard_map/ppermute | solution.py:450
  33.2 2.5 %collective-permute-done.5 = bf16[180,96]{0,1:T(8,128)(2,1)} collective-permute-done((bf16[180,96]{0,1:T(8,128)(2,1)S(1)}, bf16[180,96]{0,1:T(8,128)(2,1)}, u32[]{:S(2)}, u32[]{:S(2)}) %collective-permute-start.5) | collective-permute-done | bytes 34592 | tf_op jit(solution)/shard_map/ppermute | solution.py:329
  35.7 1.3 collective-permute-start.7
  39.5 1.1 broadcast_in_dim.14
  40.6 5.0 %all-to-all-start = ((bf16[8,180,384]{2,1,0:T(8,128)(2,1)}), bf16[8,180,384]{2,1,0:T(8,128)(2,1)S(1)}, u32[]{:S(2)}, u32[]{:S(2)}) async-start(bf16[8,180,384]{2,1,0:T(8,128)(2,1)} %broadcast_in_dim.14), calls=%async_computation | async-start | bytes 2260992 | tf_op jit(solution)/shard_map/all_to_all | solution.py:87
  45.6 9.7 %collective-permute-done.7.below_ref = bf16[14,128,128]{2,1,0:T(8,128)(2,1)S(1)} collective-permute-done((bf16[14,128,128]{2,1,0:T(8,128)(2,1)S(1)}, bf16[14,128,128]{2,1,0:T(8,128)(2,1)S(1)}, u32[]{:S(2)}, u32[]{:S(2)}) %collective-permute-start.7) | collective-permute-done | bytes 458784 | tf_op jit(solution)/shard_map/ppermute | solution.py:450
  55.5 1.9 %collective-permute-start.8 = (bf16[34,16,128]{2,1,0:T(8,128)(2,1)S(1)}, bf16[34,16,128]{2,1,0:T(8,128)(2,1)S(1)}, u32[]{:S(2)}, u32[]{:S(2)}) collective-permute-start(bf16[34,16,128]{2,1,0:T(8,128)(2,1)S(1)} %pad_maximum_fusion.2), channel_id=1, source_target_pairs={{0,1},{1,2},{2,3},{4,5},{5,6},{6,7},{8,9},{9,10},{10,11},{12,13},{... | collective-permute-start | bytes 417800 | tf_op jit(solution)/shard_map/ppermute | solution.py:450
  57.5 3.9 %collective-permute-start.9 = (bf16[34,16,128]{2,1,0:T(8,128)(2,1)S(1)}, bf16[34,16,128]{2,1,0:T(8,128)(2,1)S(1)}, u32[]{:S(2)}, u32[]{:S(2)}) collective-permute-start(bf16[34,16,128]{2,1,0:T(8,128)(2,1)S(1)} %pad_maximum_fusion.3), channel_id=1, source_target_pairs={{1,0},{2,1},{3,2},{5,4},{6,5},{7,6},{9,8},{10,9},{11,10},{13,12},{... | collective-permute-start | bytes 417800 | tf_op jit(solution)/shard_map/ppermute | solution.py:450
  61.5 1.2 reshape.119.refs_6_
  62.7 19.8 %advance_latitudes.1 = (bf16[2,360,384]{2,1,0:T(8,128)(2,1)}, bf16[2,360,384]{2,1,0:T(8,128)(2,1)}, bf16[2,360,384]{2,1,0:T(8,128)(2,1)}, bf16[2,360,384]{2,1,0:T(8,128)(2,1)}, bf16[4,32,128]{2,1,0:T(8,128)(2,1)}) custom-call(s32[3]{0:T(128)} %pad_add_fusion.1.place_ref, bf16[2,360,384]{2,1,0:T(8,128)(2,1)} %get-tuple-element.48.refs_0_, ...), custom_call_target="tpu_custom_call" | custom-call | flops 32000000000 | bytes 12582912 | tf_op jit(solution)/shard_map/advance_latitudes/pallas_call | solution.py:262
  83.3 2.6 %collective-permute-start.10 = (bf16[32,128]{1,0:T(8,128)(2,1)S(1)}, bf16[32,128]{1,0:T(8,128)(2,1)S(1)}, u32[]{:S(2)}, u32[]{:S(2)}) collective-permute-start(bf16[32,128]{1,0:T(8,128)(2,1)S(1)} %get-tuple-element.55), channel_id=1, source_target_pairs={{0,3},{1,0},{2,1},{3,2},{4,7},{5,4},{6,5},{7,6},{8,11},{9,8},{10,9... | collective-permute-start | bytes 24584 | tf_op jit(solution)/shard_map/ppermute | solution.py:329
  85.9 1.8 %collective-permute-start.11 = (bf16[32,128]{1,0:T(8,128)(2,1)S(1)}, bf16[32,128]{1,0:T(8,128)(2,1)S(1)}, u32[]{:S(2)}, u32[]{:S(2)}) collective-permute-start(bf16[32,128]{1,0:T(8,128)(2,1)S(1)} %get-tuple-element.56), channel_id=1, source_target_pairs={{0,2},{1,3},{2,0},{3,1},{4,6},{5,7},{6,4},{7,5},{8,10},{9,11},{10,... | collective-permute-start | bytes 24584 | tf_op jit(solution)/shard_map/ppermute | solution.py:329
  88.3 2.2 %collective-permute-done.11 = bf16[32,128]{1,0:T(8,128)(2,1)S(1)} collective-permute-done((bf16[32,128]{1,0:T(8,128)(2,1)S(1)}, bf16[32,128]{1,0:T(8,128)(2,1)S(1)}, u32[]{:S(2)}, u32[]{:S(2)}) %collective-permute-start.11) | collective-permute-done | bytes 8224 | tf_op jit(solution)/shard_map/ppermute | solution.py:329
  90.4 0.9 collective-permute-done.12
  91.9 3.6 %collective-permute-start.14 = (bf16[2,360,384]{2,1,0:T(8,128)(2,1)}, bf16[2,360,384]{2,1,0:T(8,128)(2,1)S(1)}, u32[]{:S(2)}, u32[]{:S(2)}) collective-permute-start(bf16[2,360,384]{2,1,0:T(8,128)(2,1)} %get-tuple-element.64), channel_id=1, source_target_pairs={{0,2},{1,3},{2,0},{3,1},{4,6},{5,7},{6,4},{7,5},{8,10},{9,11},{10,... | collective-permute-start | bytes 1658888 | tf_op jit(solution)/shard_map/ppermute | solution.py:329
  97.0 5.1 %all-to-all-start.1 = ((bf16[8,4,32,128]{3,2,1,0:T(8,128)(2,1)}), bf16[8,4,32,128]{3,2,1,0:T(8,128)(2,1)S(1)}, u32[]{:S(2)}, u32[]{:S(2)}) async-start(bf16[8,4,32,128]{3,2,1,0:T(8,128)(2,1)} %broadcast_in_dim.35), calls=%async_computation.1 | async-start | bytes 524288 | tf_op jit(solution)/shard_map/all_to_all | solution.py:87
  103.9 4.8 %all-to-all-done.1 = bf16[8,4,32,128]{3,2,1,0:T(8,128)(2,1)S(1)} async-done(((bf16[8,4,32,128]{3,2,1,0:T(8,128)(2,1)}), bf16[8,4,32,128]{3,2,1,0:T(8,128)(2,1)S(1)}, u32[]{:S(2)}, u32[]{:S(2)}) %all-to-all-start.1) | async-done | bytes 262176 | tf_op jit(solution)/shard_map/all_to_all | solution.py:87
  109.4 17.7 %denoise.1 = bf16[128,2048]{1,0:T(8,128)(2,1)} custom-call(s32[2]{0:T(128)} %pad_add_fusion.2.place_ref, s32[8]{0:T(128)} %fusion.19.pick_ref, bf16[16,128,128]{2,1,0:T(8,128)(2,1)} %copy-done, bf16[16,128,128]{2,1,0:T(8,128)(2,1)} %copy-done.1, bf16[14,128,128]{2,1,0:T(8,128)(2,1)} %copy-done.4, bf16[14,128,128]{2,1,0:T(8,128)(2,1)} %copy-done.5, ...), custom_call_target="tpu_custom_call" | custom-call | flops 1000000 | bytes 100000 | tf_op jit(solution)/shard_map/denoise/pallas_call | solution.py:657
  127.1 1.0 slice.122
  129.0 9.5 %collective-permute-done.14.refs_2_ = bf16[2,360,384]{2,1,0:T(8,128)(2,1)S(1)} collective-permute-done((bf16[2,360,384]{2,1,0:T(8,128)(2,1)}, bf16[2,360,384]{2,1,0:T(8,128)(2,1)S(1)}, u32[]{:S(2)}, u32[]{:S(2)}) %collective-permute-start.14) | collective-permute-done | bytes 552992 | tf_op jit(solution)/shard_map/ppermute | solution.py:329
  138.5 3.3 %collective-permute-done.15.refs_3_ = bf16[2,360,384]{2,1,0:T(8,128)(2,1)S(1)} collective-permute-done((bf16[2,360,384]{2,1,0:T(8,128)(2,1)}, bf16[2,360,384]{2,1,0:T(8,128)(2,1)S(1)}, u32[]{:S(2)}, u32[]{:S(2)}) %collective-permute-start.15) | collective-permute-done | bytes 552992 | tf_op jit(solution)/shard_map/ppermute | solution.py:329
  142.6 3.1 %collate.1 = bf16[8,360,384]{2,1,0:T(8,128)(2,1)} custom-call(s32[4]{0:T(128)} %pad_add_fusion.place_ref, bf16[2,360,384]{2,1,0:T(8,128)(2,1)} %get-tuple-element.81.refs_0_, bf16[2,360,384]{2,1,0:T(8,128)(2,1)} %copy-done.7, bf16[2,360,384]{2,1,0:T(8,128)(2,1)} %copy-done.8, bf16[2,360,384]{2,1,0:T(8,128)(2,1)} %copy-done.9), custom_call_target="tpu_custom_call" | custom-call | tf_op jit(solution)/shard_map/collate/pallas_call | solution.py:314
  (119 shorter events, 19.3 us)
Async XLA Ops:
  2.6 11.4 %copy-start.3 = (bf16[2,99,16,128]{3,2,1,0:T(8,128)(2,1)S(1)}, bf16[2,99,16,128]{3,2,1,0:T(8,128)(2,1)}, u32[]{:S(2)}) copy-start(bf16[2,99,16,128]{3,2,1,0:T(8,128)(2,1)} %param.26) | copy-start | bytes 2433028
  2.6 11.4 %copy-start.10 = (bf16[99,16,128]{2,1,0:T(8,128)(2,1)S(1)}, bf16[99,16,128]{2,1,0:T(8,128)(2,1)}, u32[]{:S(2)}) copy-start(bf16[99,16,128]{2,1,0:T(8,128)(2,1)} %param.25) | copy-start | bytes 1216516
  2.6 11.6 %copy-start.21 = (s32[16,128]{1,0:T(8,128)S(1)}, s32[16,128]{1,0:T(8,128)}, u32[]{:S(2)}) copy-start(s32[16,128]{1,0:T(8,128)} %param.34) | copy-start | bytes 24580
  2.6 11.7 %copy-start.22 = (s32[16,128]{1,0:T(8,128)S(1)}, s32[16,128]{1,0:T(8,128)}, u32[]{:S(2)}) copy-start(s32[16,128]{1,0:T(8,128)} %param.35) | copy-start | bytes 24580
  5.7 20.1 %collective-permute-start.3 = (bf16[180,96]{0,1:T(8,128)(2,1)S(1)}, bf16[180,96]{0,1:T(8,128)(2,1)}, u32[]{:S(2)}, u32[]{:S(2)}) collective-permute-start(bf16[180,96]{0,1:T(8,128)(2,1)S(1)} %dynamic-slice_convert_fusion), channel_id=1, source_target_pairs={{0,3},{1,0},{2,1},{3,2},{4,7},{5,4},{6,5},{7,6},{8,11},{9,8},{10,9... | collective-permute-start | bytes 103688 | tf_op jit(solution)/shard_map/ppermute | solution.py:329
  5.7 23.3 %collective-permute-start.4 = (bf16[180,96]{0,1:T(8,128)(2,1)S(1)}, bf16[180,96]{0,1:T(8,128)(2,1)}, u32[]{:S(2)}, u32[]{:S(2)}) collective-permute-start(bf16[180,96]{0,1:T(8,128)(2,1)S(1)} %dynamic-slice_convert_fusion), channel_id=1, source_target_pairs={{0,2},{1,3},{2,0},{3,1},{4,6},{5,7},{6,4},{7,5},{8,10},{9,11},{10,... | collective-permute-start | bytes 103688 | tf_op jit(solution)/shard_map/ppermute | solution.py:329
  8.7 26.9 %collective-permute-start.5 = (bf16[180,96]{0,1:T(8,128)(2,1)S(1)}, bf16[180,96]{0,1:T(8,128)(2,1)}, u32[]{:S(2)}, u32[]{:S(2)}) collective-permute-start(bf16[180,96]{0,1:T(8,128)(2,1)S(1)} %dynamic-slice_convert_fusion), channel_id=1, source_target_pairs={{0,1},{1,2},{2,3},{3,0},{4,5},{5,6},{6,7},{7,4},{8,9},{9,10},{10,1... | collective-permute-start | bytes 103688 | tf_op jit(solution)/shard_map/ppermute | solution.py:329
  11.2 50.3 %collective-permute-start = (bf16[2,360,384]{2,1,0:T(8,128)(2,1)}, bf16[2,360,384]{2,1,0:T(8,128)(2,1)}, u32[]{:S(2)}, u32[]{:S(2)}) collective-permute-start(bf16[2,360,384]{2,1,0:T(8,128)(2,1)} %get-tuple-element.45), channel_id=1, source_target_pairs={{0,3},{1,0},{2,1},{3,2},{4,7},{5,4},{6,5},{7,6},{8,11},{9,8},{10,9... | collective-permute-start | bytes 1658888 | tf_op jit(solution)/shard_map/ppermute | solution.py:329
  11.2 50.3 %collective-permute-start.1 = (bf16[2,360,384]{2,1,0:T(8,128)(2,1)}, bf16[2,360,384]{2,1,0:T(8,128)(2,1)}, u32[]{:S(2)}, u32[]{:S(2)}) collective-permute-start(bf16[2,360,384]{2,1,0:T(8,128)(2,1)} %get-tuple-element.46), channel_id=1, source_target_pairs={{0,2},{1,3},{2,0},{3,1},{4,6},{5,7},{6,4},{7,5},{8,10},{9,11},{10,... | collective-permute-start | bytes 1658888 | tf_op jit(solution)/shard_map/ppermute | solution.py:329
  15.6 4.8 %copy-start.1 = (bf16[16,128,128]{2,1,0:T(8,128)(2,1)}, bf16[16,128,128]{2,1,0:T(8,128)(2,1)S(1)}, u32[]{:S(2)}) copy-start(bf16[16,128,128]{2,1,0:T(8,128)(2,1)S(1)} %get-tuple-element.67.mid1_ref) | copy-start | bytes 1572868
  15.6 5.4 %copy-start = (bf16[16,128,128]{2,1,0:T(8,128)(2,1)}, bf16[16,128,128]{2,1,0:T(8,128)(2,1)S(1)}, u32[]{:S(2)}) copy-start(bf16[16,128,128]{2,1,0:T(8,128)(2,1)S(1)} %get-tuple-element.66.mid0_ref) | copy-start | bytes 1572868
  22.4 5.8 %copy-start.13 = (bf16[180,672]{0,1:T(8,128)(2,1)S(1)}, bf16[180,672]{0,1:T(8,128)(2,1)}, u32[]{:S(2)}) copy-start(bf16[180,672]{0,1:T(8,128)(2,1)} %constant_dynamic-update-slice_fusion.6) | copy-start | bytes 725764
  25.8 35.7 %collective-permute-start.2 = (bf16[2,360,384]{2,1,0:T(8,128)(2,1)}, bf16[2,360,384]{2,1,0:T(8,128)(2,1)S(1)}, u32[]{:S(2)}, u32[]{:S(2)}) collective-permute-start(bf16[2,360,384]{2,1,0:T(8,128)(2,1)} %get-tuple-element.47), channel_id=1, source_target_pairs={{0,1},{1,2},{2,3},{3,0},{4,5},{5,6},{6,7},{7,4},{8,9},{9,10},{10,1... | collective-permute-start | bytes 1658888 | tf_op jit(solution)/shard_map/ppermute | solution.py:329
  29.0 26.4 %collective-permute-start.6 = (bf16[14,128,128]{2,1,0:T(8,128)(2,1)}, bf16[14,128,128]{2,1,0:T(8,128)(2,1)S(1)}, u32[]{:S(2)}, u32[]{:S(2)}) collective-permute-start(bf16[14,128,128]{2,1,0:T(8,128)(2,1)} %pad_maximum_fusion), channel_id=1, source_target_pairs={{0,4},{4,8},{8,12},{12,16},{16,20},{20,24},{24,28},{1,5},{5,9},{9,... | collective-permute-start | bytes 1376264 | tf_op jit(solution)/shard_map/ppermute | solution.py:450
  35.7 19.7 %collective-permute-start.7 = (bf16[14,128,128]{2,1,0:T(8,128)(2,1)S(1)}, bf16[14,128,128]{2,1,0:T(8,128)(2,1)S(1)}, u32[]{:S(2)}, u32[]{:S(2)}) collective-permute-start(bf16[14,128,128]{2,1,0:T(8,128)(2,1)S(1)} %pad_maximum_fusion.1), channel_id=1, source_target_pairs={{4,0},{8,4},{12,8},{16,12},{20,16},{24,20},{28,24},{5,1},{9,5},{13... | collective-permute-start | bytes 1376264 | tf_op jit(solution)/shard_map/ppermute | solution.py:450
  39.5 15.8 %copy-start.17 = (bf16[16,5,128]{2,1,0:T(8,128)(2,1)S(1)}, bf16[16,5,128]{2,1,0:T(8,128)(2,1)}, u32[]{:S(2)}) copy-start(bf16[16,5,128]{2,1,0:T(8,128)(2,1)} %get-tuple-element.99) | copy-start | bytes 61444
  40.6 16.8 %copy-start.16 = (bf16[16,5,128]{2,1,0:T(8,128)(2,1)S(1)}, bf16[16,5,128]{2,1,0:T(8,128)(2,1)}, u32[]{:S(2)}) copy-start(bf16[16,5,128]{2,1,0:T(8,128)(2,1)} %get-tuple-element.98) | copy-start | bytes 61444
  40.6 20.9 %all-to-all-start = ((bf16[8,180,384]{2,1,0:T(8,128)(2,1)}), bf16[8,180,384]{2,1,0:T(8,128)(2,1)S(1)}, u32[]{:S(2)}, u32[]{:S(2)}) async-start(bf16[8,180,384]{2,1,0:T(8,128)(2,1)} %broadcast_in_dim.14), calls=%async_computation | async-start | bytes 2260992 | tf_op jit(solution)/shard_map/all_to_all | solution.py:87
  55.3 7.4 %copy-start.5 = (bf16[14,128,128]{2,1,0:T(8,128)(2,1)}, bf16[14,128,128]{2,1,0:T(8,128)(2,1)S(1)}, u32[]{:S(2)}) copy-start(bf16[14,128,128]{2,1,0:T(8,128)(2,1)S(1)} %collective-permute-done.7.below_ref) | copy-start | bytes 1376260
  55.3 7.4 %copy-start.4 = (bf16[14,128,128]{2,1,0:T(8,128)(2,1)}, bf16[14,128,128]{2,1,0:T(8,128)(2,1)S(1)}, u32[]{:S(2)}) copy-start(bf16[14,128,128]{2,1,0:T(8,128)(2,1)S(1)} %collective-permute-done.6.above_ref) | copy-start | bytes 1376260
  55.5 27.7 %collective-permute-start.8 = (bf16[34,16,128]{2,1,0:T(8,128)(2,1)S(1)}, bf16[34,16,128]{2,1,0:T(8,128)(2,1)S(1)}, u32[]{:S(2)}, u32[]{:S(2)}) collective-permute-start(bf16[34,16,128]{2,1,0:T(8,128)(2,1)S(1)} %pad_maximum_fusion.2), channel_id=1, source_target_pairs={{0,1},{1,2},{2,3},{4,5},{5,6},{6,7},{8,9},{9,10},{10,11},{12,13},{... | collective-permute-start | bytes 417800 | tf_op jit(solution)/shard_map/ppermute | solution.py:450
  57.5 25.7 %collective-permute-start.9 = (bf16[34,16,128]{2,1,0:T(8,128)(2,1)S(1)}, bf16[34,16,128]{2,1,0:T(8,128)(2,1)S(1)}, u32[]{:S(2)}, u32[]{:S(2)}) collective-permute-start(bf16[34,16,128]{2,1,0:T(8,128)(2,1)S(1)} %pad_maximum_fusion.3), channel_id=1, source_target_pairs={{1,0},{2,1},{3,2},{5,4},{6,5},{7,6},{9,8},{10,9},{11,10},{13,12},{... | collective-permute-start | bytes 417800 | tf_op jit(solution)/shard_map/ppermute | solution.py:450
  83.2 25.4 %copy-start.14 = (bf16[34,16,128]{2,1,0:T(8,128)(2,1)}, bf16[34,16,128]{2,1,0:T(8,128)(2,1)S(1)}, u32[]{:S(2)}) copy-start(bf16[34,16,128]{2,1,0:T(8,128)(2,1)S(1)} %collective-permute-done.8.left_ref) | copy-start | bytes 417796
  83.3 25.4 %copy-start.15 = (bf16[34,16,128]{2,1,0:T(8,128)(2,1)}, bf16[34,16,128]{2,1,0:T(8,128)(2,1)S(1)}, u32[]{:S(2)}) copy-start(bf16[34,16,128]{2,1,0:T(8,128)(2,1)S(1)} %collective-permute-done.9.right_ref) | copy-start | bytes 417796
  83.3 5.0 %collective-permute-start.10 = (bf16[32,128]{1,0:T(8,128)(2,1)S(1)}, bf16[32,128]{1,0:T(8,128)(2,1)S(1)}, u32[]{:S(2)}, u32[]{:S(2)}) collective-permute-start(bf16[32,128]{1,0:T(8,128)(2,1)S(1)} %get-tuple-element.55), channel_id=1, source_target_pairs={{0,3},{1,0},{2,1},{3,2},{4,7},{5,4},{6,5},{7,6},{8,11},{9,8},{10,9... | collective-permute-start | bytes 24584 | tf_op jit(solution)/shard_map/ppermute | solution.py:329
  85.9 4.5 %collective-permute-start.11 = (bf16[32,128]{1,0:T(8,128)(2,1)S(1)}, bf16[32,128]{1,0:T(8,128)(2,1)S(1)}, u32[]{:S(2)}, u32[]{:S(2)}) collective-permute-start(bf16[32,128]{1,0:T(8,128)(2,1)S(1)} %get-tuple-element.56), channel_id=1, source_target_pairs={{0,2},{1,3},{2,0},{3,1},{4,6},{5,7},{6,4},{7,5},{8,10},{9,11},{10,... | collective-permute-start | bytes 24584 | tf_op jit(solution)/shard_map/ppermute | solution.py:329
  87.7 3.7 %collective-permute-start.12 = (bf16[32,128]{1,0:T(8,128)(2,1)S(1)}, bf16[32,128]{1,0:T(8,128)(2,1)S(1)}, u32[]{:S(2)}, u32[]{:S(2)}) collective-permute-start(bf16[32,128]{1,0:T(8,128)(2,1)S(1)} %get-tuple-element.57), channel_id=1, source_target_pairs={{0,1},{1,2},{2,3},{3,0},{4,5},{5,6},{6,7},{7,4},{8,9},{9,10},{10,1... | collective-permute-start | bytes 24584 | tf_op jit(solution)/shard_map/ppermute | solution.py:329
  91.3 37.7 %collective-permute-start.13 = (bf16[2,360,384]{2,1,0:T(8,128)(2,1)}, bf16[2,360,384]{2,1,0:T(8,128)(2,1)S(1)}, u32[]{:S(2)}, u32[]{:S(2)}) collective-permute-start(bf16[2,360,384]{2,1,0:T(8,128)(2,1)} %get-tuple-element.63), channel_id=1, source_target_pairs={{0,1},{1,2},{2,3},{3,0},{4,5},{5,6},{6,7},{7,4},{8,9},{9,10},{10,1... | collective-permute-start | bytes 1658888 | tf_op jit(solution)/shard_map/ppermute | solution.py:329
  91.9 46.6 %collective-permute-start.14 = (bf16[2,360,384]{2,1,0:T(8,128)(2,1)}, bf16[2,360,384]{2,1,0:T(8,128)(2,1)S(1)}, u32[]{:S(2)}, u32[]{:S(2)}) collective-permute-start(bf16[2,360,384]{2,1,0:T(8,128)(2,1)} %get-tuple-element.64), channel_id=1, source_target_pairs={{0,2},{1,3},{2,0},{3,1},{4,6},{5,7},{6,4},{7,5},{8,10},{9,11},{10,... | collective-permute-start | bytes 1658888 | tf_op jit(solution)/shard_map/ppermute | solution.py:329
  95.6 46.2 %collective-permute-start.15 = (bf16[2,360,384]{2,1,0:T(8,128)(2,1)}, bf16[2,360,384]{2,1,0:T(8,128)(2,1)S(1)}, u32[]{:S(2)}, u32[]{:S(2)}) collective-permute-start(bf16[2,360,384]{2,1,0:T(8,128)(2,1)} %get-tuple-element.65), channel_id=1, source_target_pairs={{0,3},{1,0},{2,1},{3,2},{4,7},{5,4},{6,5},{7,6},{8,11},{9,8},{10,9... | collective-permute-start | bytes 1658888 | tf_op jit(solution)/shard_map/ppermute | solution.py:329
  97.0 11.7 %all-to-all-start.1 = ((bf16[8,4,32,128]{3,2,1,0:T(8,128)(2,1)}), bf16[8,4,32,128]{3,2,1,0:T(8,128)(2,1)S(1)}, u32[]{:S(2)}, u32[]{:S(2)}) async-start(bf16[8,4,32,128]{3,2,1,0:T(8,128)(2,1)} %broadcast_in_dim.35), calls=%async_computation.1 | async-start | bytes 524288 | tf_op jit(solution)/shard_map/all_to_all | solution.py:87
  129.0 12.7 %copy-start.7 = (bf16[2,360,384]{2,1,0:T(8,128)(2,1)}, bf16[2,360,384]{2,1,0:T(8,128)(2,1)S(1)}, u32[]{:S(2)}) copy-start(bf16[2,360,384]{2,1,0:T(8,128)(2,1)S(1)} %collective-permute-done.13.refs_1_) | copy-start | bytes 1658884
  (10 other events, 19.3 us)
